TPU v7x, 256 devices: a whole 4x4x8 slice. The times are simulated.
256 devices in a mesh: grp: 32 (over z, y_hi, core), blk: 8 (over x, y_lo).
Axes of the slice: x: 4, y: 4 (y_hi: 2, y_lo: 2; y = y_hi * 2 + y_lo), z: 8, core: 2. Of those that a mesh axis runs over, the one named last changes fastest.
Arguments:
- samples: bfloat16 [8, 256, 268288], P('blk', 'grp'), may hold values from -7 to 7, as said below
- input_gains: float32 [8, 256, 256], P('blk', 'grp'), may hold values from 0.5 to 2
Outputs:
- vis_near: bfloat16 [4, 256, 2, 2048, 256], P(None, 'grp', None, 'blk')
- vis_far: bfloat16 [128, 2, 2048, 256], P('grp', None, 'blk')
Inputs may be any that keep to these rules, and one draw needn't show every extreme that they name: `samples`: whole numbers.
All inputs are finite; a program needn't handle non-finite values.
Results may differ from a plain program's by a relative error of at most 0.0054.
Values may be sent and summed in bfloat16 or wider, within the bound.
No kernel may reach another device: no remote copies, remote signals or barrier semaphores. Data moves between devices by JAX's collectives and lax.ppermute only.
A program may use at most 128 MiB of HBM per device.

v0:
```python
import math

import jax
import jax.numpy as jnp
from jax import lax
from jax.sharding import PartitionSpec as P

TAPS = 4
BAND = 256
SPEC = 128
FRAME = 2048


def passed_along(block, axis, distance):
    devices = range(lax.axis_size(axis))
    route = [((i - distance) % len(devices), i) for i in devices]
    return lax.ppermute(block, axis, route)


def prototype_taps():
    length_all = TAPS * FRAME
    position_frac = (jnp.arange(length_all, dtype=jnp.float32) + 0.5) / length_all
    hann_window = 0.5 - 0.5 * jnp.cos(2.0 * jnp.pi * position_frac)
    return (jnp.sinc(TAPS * (position_frac - 0.5)) * hann_window).reshape(TAPS, FRAME)


def channel_table(channels):
    sample_index = jnp.arange(FRAME, dtype=jnp.int32)[:, None]
    channel_index = BAND + jnp.arange(channels, dtype=jnp.int32)[None, :]
    phase_index = sample_index * channel_index % FRAME
    angles = phase_index.astype(jnp.float32) * (2.0 * jnp.pi / FRAME)
    factor = 0.25 / math.sqrt(FRAME)
    stacked = jnp.stack([jnp.cos(angles) * factor, -jnp.sin(angles) * factor], axis=2)
    return stacked.reshape(FRAME, 2 * channels).astype(jnp.bfloat16)


def filter_frames(voltages, spectra_count):
    row_count = voltages.shape[0]
    framed = voltages.reshape(row_count, spectra_count + TAPS - 1, FRAME)
    weights = prototype_taps()
    summed = jnp.zeros((row_count, spectra_count, FRAME), jnp.float32)
    for tap_index in range(TAPS):
        summed = summed + weights[tap_index] * framed[
            :, tap_index : tap_index + spectra_count, :
        ].astype(jnp.float32)
    return summed.astype(jnp.bfloat16)


def correlate_pair(own_block, other_block, inverse):
    products = jnp.einsum(
        "cais,cbjs->caibj", own_block, other_block, preferred_element_type=jnp.float32
    )
    real_part = products[:, 0, :, 0, :] + products[:, 1, :, 1, :]
    imag_part = products[:, 1, :, 0, :] - products[:, 0, :, 1, :]
    return (jnp.stack([real_part, imag_part], axis=1) * inverse).astype(jnp.bfloat16)


def channel_half(block_spectra, position, blocks_total, half_count):
    pair_width = block_spectra.shape[0] // 2
    start_row = position % blocks_total // half_count * pair_width
    return lax.dynamic_slice_in_dim(block_spectra, start_row, pair_width, 0)


def on_device(samples, input_gains):
    spectra_count = SPEC
    share_rows = samples.shape[1]
    channels = input_gains.shape[2]
    voltages = samples.reshape(share_rows, samples.shape[2])
    frames = filter_frames(voltages, spectra_count)
    dft_table = channel_table(channels)
    raw_spectra = lax.dot_general(
        dft_table, frames, (((0,), (2,)), ((), ())), preferred_element_type=jnp.float32
    )
    raw_spectra = raw_spectra.reshape(channels, 2, share_rows, spectra_count)
    channel_gains = jnp.transpose(input_gains[0])[:, None, :, None]
    local_spectra = (raw_spectra * channel_gains).astype(jnp.bfloat16)
    own_block = lax.all_to_all(local_spectra, "grp", split_axis=0, concat_axis=2, tiled=True)
    blocks_total = lax.axis_size("blk")
    half_count = blocks_total // 2
    position = lax.axis_index("blk")
    inverse = 1.0 / spectra_count
    near_list = [correlate_pair(own_block, own_block, inverse)]
    passing = own_block
    for offset in range(1, half_count):
        passing = passed_along(passing, "blk", -1)
        near_list.append(correlate_pair(own_block, passing, inverse))
    outgoing = channel_half(passing, position - 1, blocks_total, half_count)
    arrived = passed_along(outgoing, "blk", -1)
    mine_half = channel_half(own_block, position, blocks_total, half_count)
    vis_far = correlate_pair(mine_half, arrived, inverse)
    return (jnp.stack(near_list, axis=0), vis_far)


def solution(mesh):
    return jax.shard_map(
        on_device,
        mesh=mesh,
        in_specs=(P("blk", "grp", None), P("blk", "grp", None)),
        out_specs=(P(None, "grp", None, "blk", None), P("grp", None, "blk", None)),
        check_vma=False,
    )
```

profile of v0, /device:TPU:48, one launch (start us, length us, event | category | flops | bytes accessed | tf_op | source)
XLA Modules:
  0.0 204.9 jit_solution(6772726955326323240)
XLA Ops:
  0.8 12.2 %fusion.62 = (bf16[8,128,2048]{2,0,1:T(8,128)(2,1)}, bf16[8,128,2048]{2,0,1:T(8,128)(2,1)}, bf16[8,128,2048]{2,0,1:T(8,128)(2,1)}, bf16[8,128,2048]{2,0,1:T(8,128)(2,1)}) fusion(bf16[8,131,2048]{2,0,1:T(8,128)(2,1)} %bitcast.92), kind=kLoop, calls=%fused_computation.98 | loop fusion | bytes 33554432 | tf_op jit(solution)/shard_map/slice | solution.py:43
  13.0 8.7 %multiply_convert_fusion.2 = (bf16[2048,256,1]{1,0,2:T(8,128)(2,1)S(1)}, bf16[2048,256,1]{1,0,2:T(8,128)(2,1)S(1)}) fusion(s32[256]{0:T(256)S(1)} %iota_add_fusion), kind=kLoop, calls=%fused_computation.42 | loop fusion | flops 9961472 | bytes 2098176 | tf_op jit(solution)/shard_map/convert
  21.9 4.1 %copy.76 = bf16[2048,256,2]{0,2,1:T(2,128)(2,1)} copy(bf16[2048,256,2]{1,0,2:T(8,128)(2,1)S(1)} %pad_maximum_fusion.1) | data formatting | bytes 4194304 | tf_op jit(solution)/shard_map/stack | solution.py:33
  26.0 2.7 %convert_element_type.87 = bf16[2048,512]{0,1:T(8,128)(2,1)S(1)} reshape(bf16[2048,256,2]{0,2,1:T(2,128)(2,1)} %copy.76) | data formatting | bytes 4194304 | tf_op jit(solution)/shard_map/convert_element_type | solution.py:34
  28.8 2.8 %dot_general.23 = bf16[256,2,2048]{2,1,0:T(2,128)(2,1)} reshape(bf16[512,2048]{1,0:T(8,128)(2,1)S(1)} %bitcast.100) | data formatting | bytes 4194304 | tf_op jit(solution)/shard_map/dot_general | solution.py:71
  31.6 33.7 %multiply_convert_fusion = bf16[256,2,8,128]{3,0,2,1:T(8,128)(2,1)S(1)} fusion(bf16[8,128,2048]{2,0,1:T(8,128)(2,1)} %get-tuple-element.19, bf16[8,128,2048]{2,0,1:T(8,128)(2,1)} %get-tuple-element.17, bf16[8,128,2048]{2,0,1:T(8,128)(2,1)} %get-tuple-element.18, bf16[8,128,2048]{2,0,1:T(8,128)(2,1)} %get-tuple-element.16, f32[2048]{0:T(1024)S(1)} %get-tuple-element.23, ...), kind=kOutput, calls=%fused_computation.40 | convolution fusion | flops 2173698048 | bytes 19963904 | tf_op jit(solution)/shard_map/dot_general | solution.py:71
  65.9 39.0 %all_to_all.18 = bf16[256,2,8,128]{3,2,1,0:T(8,128)(2,1)S(1)} all-to-all(bf16[256,2,8,128]{3,2,1,0:T(8,128)(2,1)S(1)} %copy.82), channel_id=1, replica_groups=mesh['grp'=32,'blk'=8] {'grp'}, dimensions={0} | all-to-all | bytes 2097152 | tf_op jit(solution)/shard_map/all_to_all | solution.py:77
  105.2 3.6 %collective-permute-start = (bf16[8,2,256,128]{3,2,1,0:T(8,128)(2,1)S(1)}, bf16[8,2,256,128]{3,2,1,0:T(8,128)(2,1)S(1)}, u32[]{:S(2)}, u32[]{:S(2)}) collective-permute-start(bf16[8,2,256,128]{3,2,1,0:T(8,128)(2,1)S(1)} %bitcast.93), channel_id=1, source_target_pairs={{1,0},{2,1},{3,2},{4,3},{5,4},{6,5},{7,6},{0,7},{9,8},{10,9},{11,1... | collective-permute-start | bytes 3145736 | tf_op jit(solution)/shard_map/ppermute | solution.py:17
  108.8 1.3 fusion.31
  110.3 21.0 %collective-permute-done = bf16[8,2,256,128]{3,2,1,0:T(8,128)(2,1)S(1)} collective-permute-done((bf16[8,2,256,128]{3,2,1,0:T(8,128)(2,1)S(1)}, bf16[8,2,256,128]{3,2,1,0:T(8,128)(2,1)S(1)}, u32[]{:S(2)}, u32[]{:S(2)}) %collective-permute-start) | collective-permute-done | bytes 1048608 | tf_op jit(solution)/shard_map/ppermute | solution.py:17
  131.3 4.6 %collective-permute-start.1 = (bf16[8,2,256,128]{3,2,1,0:T(8,128)(2,1)S(1)}, bf16[8,2,256,128]{3,2,1,0:T(8,128)(2,1)S(1)}, u32[]{:S(2)}, u32[]{:S(2)}) collective-permute-start(bf16[8,2,256,128]{3,2,1,0:T(8,128)(2,1)S(1)} %collective-permute-done), channel_id=1, source_target_pairs={{1,0},{2,1},{3,2},{4,3},{5,4},{6,5},{7,6},{0,7},{9,8},{10,9},{11,1... | collective-permute-start | bytes 3145736 | tf_op jit(solution)/shard_map/ppermute | solution.py:17
  136.2 1.3 fusion.38
  138.1 19.5 %collective-permute-done.1 = bf16[8,2,256,128]{3,2,1,0:T(8,128)(2,1)S(1)} collective-permute-done((bf16[8,2,256,128]{3,2,1,0:T(8,128)(2,1)S(1)}, bf16[8,2,256,128]{3,2,1,0:T(8,128)(2,1)S(1)}, u32[]{:S(2)}, u32[]{:S(2)}) %collective-permute-start.1) | collective-permute-done | bytes 1048608 | tf_op jit(solution)/shard_map/ppermute | solution.py:17
  157.6 4.6 %collective-permute-start.2 = (bf16[8,2,256,128]{3,2,1,0:T(8,128)(2,1)S(1)}, bf16[8,2,256,128]{3,2,1,0:T(8,128)(2,1)S(1)}, u32[]{:S(2)}, u32[]{:S(2)}) collective-permute-start(bf16[8,2,256,128]{3,2,1,0:T(8,128)(2,1)S(1)} %collective-permute-done.1), channel_id=1, source_target_pairs={{1,0},{2,1},{3,2},{4,3},{5,4},{6,5},{7,6},{0,7},{9,8},{10,9},{11,1... | collective-permute-start | bytes 3145736 | tf_op jit(solution)/shard_map/ppermute | solution.py:17
  162.2 1.1 fusion.1
  163.3 1.3 fusion.36
  165.2 17.8 %collective-permute-done.2 = bf16[8,2,256,128]{3,2,1,0:T(8,128)(2,1)S(1)} collective-permute-done((bf16[8,2,256,128]{3,2,1,0:T(8,128)(2,1)S(1)}, bf16[8,2,256,128]{3,2,1,0:T(8,128)(2,1)S(1)}, u32[]{:S(2)}, u32[]{:S(2)}) %collective-permute-start.2) | collective-permute-done | bytes 1048608 | tf_op jit(solution)/shard_map/ppermute | solution.py:17
  183.0 4.8 %collective-permute-start.3 = (bf16[4,2,256,128]{3,2,1,0:T(8,128)(2,1)S(1)}, bf16[4,2,256,128]{3,2,1,0:T(8,128)(2,1)S(1)}, u32[]{:S(2)}, u32[]{:S(2)}) collective-permute-start(bf16[4,2,256,128]{3,2,1,0:T(8,128)(2,1)S(1)} %constant_dynamic-slice_fusion), channel_id=1, source_target_pairs={{1,0},{2,1},{3,2},{4,3},{5,4},{6,5},{7,6},{0,7},{9,8},{10,9},{11,1... | collective-permute-start | bytes 1572872 | tf_op jit(solution)/shard_map/ppermute | solution.py:17
  187.8 1.3 fusion.34
  189.7 1.1 fusion.3
  190.8 3.8 %pad_maximum_fusion = bf16[4,8,2,256,256]{4,3,1,2,0:T(8,128)(2,1)} fusion(bf16[1,8,2,256,256]{4,3,1,2,0:T(8,128)(2,1)S(1)} %get-tuple-element.31, bf16[1,8,2,256,256]{4,3,1,2,0:T(8,128)(2,1)S(1)} %get-tuple-element.30, bf16[1,8,2,256,256]{4,3,1,2,0:T(8,128)(2,1)S(1)} %get-tuple-element.29, bf16[1,8,2,256,256]{4,3,1,2,0:T(8,128)(2,1)S(1)} %get-tuple-element.28), kind=kLoop, calls=%fused_computation | loop fusion | flops 12582912 | bytes 16777216 | tf_op jit(solution)/shard_map/stack | solution.py:91
  194.7 7.8 %copy.100 = bf16[4,8,2,256,256]{4,3,2,1,0:T(8,128)(2,1)} copy(bf16[4,8,2,256,256]{4,3,1,2,0:T(8,128)(2,1)} %pad_maximum_fusion) | data formatting | bytes 16777216
  202.4 0.7 fusion.44
  203.7 1.0 copy.101
  (18 shorter events, 4.3 us)
Async XLA Ops:
  28.7 2.8 %copy-start = (f32[1,8,256]{2,1,0:T(8,128)S(1)}, f32[1,8,256]{2,1,0:T(8,128)}, u32[]{:S(2)}) copy-start(f32[1,8,256]{2,1,0:T(8,128)} %param.3) | copy-start | bytes 24580
  105.2 26.1 %collective-permute-start = (bf16[8,2,256,128]{3,2,1,0:T(8,128)(2,1)S(1)}, bf16[8,2,256,128]{3,2,1,0:T(8,128)(2,1)S(1)}, u32[]{:S(2)}, u32[]{:S(2)}) collective-permute-start(bf16[8,2,256,128]{3,2,1,0:T(8,128)(2,1)S(1)} %bitcast.93), channel_id=1, source_target_pairs={{1,0},{2,1},{3,2},{4,3},{5,4},{6,5},{7,6},{0,7},{9,8},{10,9},{11,1... | collective-permute-start | bytes 3145736 | tf_op jit(solution)/shard_map/ppermute | solution.py:17
  131.3 26.3 %collective-permute-start.1 = (bf16[8,2,256,128]{3,2,1,0:T(8,128)(2,1)S(1)}, bf16[8,2,256,128]{3,2,1,0:T(8,128)(2,1)S(1)}, u32[]{:S(2)}, u32[]{:S(2)}) collective-permute-start(bf16[8,2,256,128]{3,2,1,0:T(8,128)(2,1)S(1)} %collective-permute-done), channel_id=1, source_target_pairs={{1,0},{2,1},{3,2},{4,3},{5,4},{6,5},{7,6},{0,7},{9,8},{10,9},{11,1... | collective-permute-start | bytes 3145736 | tf_op jit(solution)/shard_map/ppermute | solution.py:17
  157.6 25.4 %collective-permute-start.2 = (bf16[8,2,256,128]{3,2,1,0:T(8,128)(2,1)S(1)}, bf16[8,2,256,128]{3,2,1,0:T(8,128)(2,1)S(1)}, u32[]{:S(2)}, u32[]{:S(2)}) collective-permute-start(bf16[8,2,256,128]{3,2,1,0:T(8,128)(2,1)S(1)} %collective-permute-done.1), channel_id=1, source_target_pairs={{1,0},{2,1},{3,2},{4,3},{5,4},{6,5},{7,6},{0,7},{9,8},{10,9},{11,1... | collective-permute-start | bytes 3145736 | tf_op jit(solution)/shard_map/ppermute | solution.py:17
  183.0 19.4 %collective-permute-start.3 = (bf16[4,2,256,128]{3,2,1,0:T(8,128)(2,1)S(1)}, bf16[4,2,256,128]{3,2,1,0:T(8,128)(2,1)S(1)}, u32[]{:S(2)}, u32[]{:S(2)}) collective-permute-start(bf16[4,2,256,128]{3,2,1,0:T(8,128)(2,1)S(1)} %constant_dynamic-slice_fusion), channel_id=1, source_target_pairs={{1,0},{2,1},{3,2},{4,3},{5,4},{6,5},{7,6},{0,7},{9,8},{10,9},{11,1... | collective-permute-start | bytes 1572872 | tf_op jit(solution)/shard_map/ppermute | solution.py:17
where the time goes:
time: 208 us; the launch traced here: 205 us
  waiting for transfers between devices  58.3 us (28%)
  matrix products  39.4 us (19%)
  blocking collectives  39 us (19%)
  local copies, waits for them, and re-layouts  31.6 us (15%)
  other arithmetic  18 us (9%)
  starting transfers between devices  17.6 us (8%)
    ppermute x4, waiting for transfers between devices, passed_along(): return lax.ppermute(block, axis, route)  58.3 us
    all_to_all x1, blocking collectives, on_device(): lax.all_to_all(local_spectra, 'grp', split_axis=0, concat_axis=2, tiled=T...  39 us
    dot_general x1, matrix products, on_device(): lax.dot_general(dft_table, frames, (((0,), (2,)), ((), ())), preferred_el...  33.7 us
    ppermute x4, starting transfers between devices, passed_along(): return lax.ppermute(block, axis, route)  17.6 us
    slice x1, local copies, waits for them, and re-layouts, filter_frames(): framed[:, tap_index:tap_index + spectra_count, :].astype(jnp.float32)  12.2 us
    unnamed x4, local copies, waits for them, and re-layouts  8.82 us
    another operation x1, other arithmetic  8.69 us
    dot_general x5, matrix products, correlate_pair(): jnp.einsum('cais,cbjs->caibj', own_block, other_block, preferred_element_...  5.72 us
  transfers between devices with their start and end apart: 4, of which 3 were waited for; matrix products, arithmetic and copies ran while one was open for 10% of the time, Pallas kernels for 0%

commit v1 on v0

v1 whole, which is shorter than its diff:
```python
import math

import jax
import jax.numpy as jnp
import numpy as np
from jax import lax
from jax.experimental import pallas as pl
from jax.experimental.pallas import tpu as pltpu
from jax.sharding import PartitionSpec as P

TAPS = 4
BAND = 256
SPEC = 128
FRAME = 2048
GROUPS = 32
PER = 8
SHARE = 8
ROWS = GROUPS * 2 * PER
LANES = 2 * SPEC
MIB = 1024 * 1024


def prototype_taps():
    position = (np.arange(TAPS * FRAME, dtype=np.float64) + 0.5) / (TAPS * FRAME)
    window = 0.5 - 0.5 * np.cos(2.0 * np.pi * position)
    return (np.sinc(TAPS * (position - 0.5)) * window).reshape(TAPS, FRAME).astype(np.float32)


def channel_table():
    phase = (np.arange(FRAME)[None, :] * (BAND + np.arange(GROUPS * PER))[:, None]) % FRAME
    angles = phase * (2.0 * np.pi / FRAME)
    factor = 0.25 / math.sqrt(FRAME)
    parts = np.stack([np.cos(angles) * factor, -np.sin(angles) * factor], axis=0)
    table = parts.reshape(2, GROUPS, PER, FRAME).transpose(1, 0, 2, 3).reshape(ROWS, FRAME)
    return table.astype(np.float32).astype(jnp.bfloat16)


SAMPLE_CUTS = (0, 19, 35, 51, 67, 83, 99, 115, 131)
COL = 128


def channelize_kernel(samples, table, taps, gains, out, held, rows, frames, turned, sem_in, sem_table):
    parts = len(SAMPLE_CUTS) - 1

    def sample_copy(i):
        span = pl.ds(SAMPLE_CUTS[i], SAMPLE_CUTS[i + 1] - SAMPLE_CUTS[i])
        return pltpu.make_async_copy(samples.at[span], held.at[span], sem_in.at[i])

    table_copy = pltpu.make_async_copy(table, rows, sem_table)
    for i in range(parts):
        sample_copy(i).start()
    table_copy.start()
    for i in range(parts):
        sample_copy(i).wait()
        first = 16 * i

        def one_column(f, carry, first=first):
            lanes = pl.ds(pl.multiple_of(f * COL, COL), COL)
            weights = [jnp.broadcast_to(taps[t : t + 1, lanes], (SHARE, COL)) for t in range(TAPS)]
            window = [held[first + t, :, lanes].astype(jnp.float32) for t in range(TAPS - 1)]
            for s in range(16):
                window.append(held[first + s + TAPS - 1, :, lanes].astype(jnp.float32))
                total = weights[0] * window[0]
                for t in range(1, TAPS):
                    total = total + weights[t] * window[t]
                frames[f, (first + s) * SHARE : (first + s + 1) * SHARE, :] = total
                window = window[1:]
            return carry

        lax.fori_loop(0, FRAME // COL, one_column, 0)
    table_copy.wait()
    scale = jnp.transpose(gains[...])
    for pair in range(SHARE // 2):
        chosen = [
            jnp.concatenate(
                [
                    frames[f, pl.ds(2 * pair + j, SPEC, stride=SHARE), :].astype(jnp.bfloat16)
                    for f in range(FRAME // COL)
                ],
                axis=1,
            )
            for j in range(2)
        ]
        spectra = lax.dot_general(
            rows[...],
            jnp.concatenate(chosen, axis=0),
            (((1,), (1,)), ((), ())),
            preferred_element_type=jnp.float32,
        )
        for j in range(2):
            n = 2 * pair + j
            factor = scale[:, n : n + 1].reshape(GROUPS, 1, PER, 1)
            mine = spectra[:, j * SPEC : (j + 1) * SPEC].reshape(GROUPS, 2, PER, SPEC) * factor
            turned[pl.ds(n, ROWS, stride=SHARE), :] = mine.reshape(ROWS, SPEC)
    whole = turned[...].reshape(GROUPS, 2, PER, SHARE, SPEC)
    for r in range(2):
        out[:, :, :, r * SPEC : (r + 1) * SPEC] = whole[:, r].astype(jnp.bfloat16)


def channelize(samples, gains):
    by_frame = jnp.transpose(samples.reshape(SHARE, SPEC + TAPS - 1, FRAME), (1, 0, 2))
    return pl.pallas_call(
        channelize_kernel,
        out_shape=jax.ShapeDtypeStruct((GROUPS, PER, SHARE, LANES), jnp.bfloat16),
        in_specs=[
            pl.BlockSpec(memory_space=pl.ANY),
            pl.BlockSpec(memory_space=pl.ANY),
            pl.BlockSpec(memory_space=pltpu.VMEM),
            pl.BlockSpec(memory_space=pltpu.VMEM),
        ],
        out_specs=pl.BlockSpec(memory_space=pltpu.VMEM),
        scratch_shapes=[
            pltpu.VMEM((SPEC + TAPS - 1, SHARE, FRAME), jnp.bfloat16),
            pltpu.VMEM((ROWS, FRAME), jnp.bfloat16),
            pltpu.VMEM((FRAME // COL, SPEC * SHARE, COL), jnp.float32),
            pltpu.VMEM((ROWS * SHARE, SPEC), jnp.float32),
            pltpu.SemaphoreType.DMA((len(SAMPLE_CUTS) - 1,)),
            pltpu.SemaphoreType.DMA,
        ],
        compiler_params=pltpu.CompilerParams(vmem_limit_bytes=58 * MIB),
        name="channelize",
    )(by_frame, channel_table(), prototype_taps(), gains)


def correlate_one(own, other, out):
    mine = own[0]
    crossed = jnp.concatenate([mine[:, SPEC:], -mine[:, :SPEC]], axis=1)
    contract = (((1,), (1,)), ((), ()))
    real = lax.dot_general(mine, other, contract, preferred_element_type=jnp.float32)
    imag = lax.dot_general(crossed, other, contract, preferred_element_type=jnp.float32)
    return real * (1.0 / SPEC), imag * (1.0 / SPEC)


def near_kernel(own, other, *rest):
    out = rest[-1]
    real, imag = correlate_one(own, other[0], out)
    out[0, 0, 0] = real.astype(jnp.bfloat16)
    out[0, 0, 1] = imag.astype(jnp.bfloat16)


def near(own, other, offset, half_count, before):
    channels, width, lanes = own.shape
    block = pl.BlockSpec((1, width, lanes), lambda c: (c, 0, 0))
    operands, specs, aliases = [own, other], [block, block], {}
    if before is not None:
        operands.append(before)
        specs.append(pl.BlockSpec(memory_space=pl.ANY))
        aliases = {2: 0}
    flops = 2 * channels * 2 * width * width * lanes
    return pl.pallas_call(
        near_kernel,
        grid=(channels,),
        out_shape=jax.ShapeDtypeStruct((half_count, channels, 2, width, width), jnp.bfloat16),
        in_specs=specs,
        out_specs=pl.BlockSpec((1, 1, 2, width, width), lambda c: (offset, c, 0, 0, 0)),
        input_output_aliases=aliases,
        cost_estimate=pl.CostEstimate(
            flops=flops, bytes_accessed=2 * own.size * 2 + channels * 4 * width * width, transcendentals=0
        ),
        compiler_params=pltpu.CompilerParams(vmem_limit_bytes=16 * MIB),
        name="near%d" % offset,
    )(*operands)


def far_kernel(start, own, other, out):
    real, imag = correlate_one(own, other[0], out)
    out[0, 0] = real.astype(jnp.bfloat16)
    out[0, 1] = imag.astype(jnp.bfloat16)


def far(own, other, start):
    channels, width, lanes = other.shape
    return pl.pallas_call(
        far_kernel,
        grid_spec=pltpu.PrefetchScalarGridSpec(
            num_scalar_prefetch=1,
            grid=(channels,),
            in_specs=[
                pl.BlockSpec((1, width, lanes), lambda c, start: (start[0] + c, 0, 0)),
                pl.BlockSpec((1, width, lanes), lambda c, start: (c, 0, 0)),
            ],
            out_specs=pl.BlockSpec((1, 2, width, width), lambda c, start: (c, 0, 0, 0)),
        ),
        out_shape=jax.ShapeDtypeStruct((channels, 2, width, width), jnp.bfloat16),
        compiler_params=pltpu.CompilerParams(vmem_limit_bytes=16 * MIB),
        name="far",
    )(start.reshape(1), own, other)


def blk_route(step):
    return [(2 * x + l, step(x, l)) for x in range(4) for l in range(2)]


LEFT = blk_route(lambda x, l: 2 * ((x - 1) % 4) + l)
RIGHT = blk_route(lambda x, l: 2 * ((x + 1) % 4) + l)
SWAP = blk_route(lambda x, l: 2 * x + 1 - l)
BACK = blk_route(lambda x, l: (2 * x + l - 1) % 8)
LEFT_ODD = blk_route(lambda x, l: 2 * ((x - l) % 4) + l)


def on_device(samples, input_gains):
    half_count = lax.axis_size("blk") // 2
    half = PER // 2
    position = lax.axis_index("blk")
    mine_start = position // half_count * half
    pieces = channelize(samples[0], input_gains[0])
    pieces = lax.all_to_all(pieces, "grp", split_axis=0, concat_axis=0, tiled=True)
    own = jnp.transpose(pieces, (1, 0, 2, 3)).reshape(PER, GROUPS * SHARE, LANES)
    outgoing = lax.dynamic_slice_in_dim(own, half - mine_start, half, 0)
    second = lax.ppermute(own, "blk", LEFT)
    across = lax.ppermute(own, "blk", SWAP)
    passing = lax.ppermute(outgoing, "blk", RIGHT)
    third = lax.ppermute(second, "blk", BACK)
    first = lax.ppermute(across, "blk", LEFT_ODD)
    arrived = lax.ppermute(passing, "blk", RIGHT)
    vis_near = near(own, own, 0, half_count, None)
    vis_near = near(own, second, 2, half_count, vis_near)
    vis_near = near(own, first, 1, half_count, vis_near)
    vis_near = near(own, third, 3, half_count, vis_near)
    vis_far = far(own, arrived, mine_start)
    return (vis_near, vis_far)


def solution(mesh):
    return jax.shard_map(
        on_device,
        mesh=mesh,
        in_specs=(P("blk", "grp", None), P("blk", "grp", None)),
        out_specs=(P(None, "grp", None, "blk", None), P("grp", None, "blk", None)),
        check_vma=False,
    )
```

time: 208 us -> 110 us (0.53)
  matrix products: 39.4 us -> 0 us
  local copies, waits for them, and re-layouts: 31.6 us -> 0.1 us
  waiting for transfers between devices: 58.3 us -> 29.7 us
  Pallas kernels: 0 us -> 27.6 us
  other arithmetic: 18 us -> 0 us
  starting transfers between devices: 17.6 us -> 11.2 us
    dot_general x6 -> x0, matrix products: 39.4 us -> none  [the longest x1 33.7 us: on_device(): lax.dot_general(dft_table, frames, (((0,), (2,)), ((), ())), preferred_el...]
    ppermute x4 -> x6, waiting for transfers between devices: 58.3 us -> 29.7 us  [the longest x1 20.9 us: on_device(): across = lax.ppermute(own, 'blk', SWAP)]
    pallas_call x0 -> x6, Pallas kernels: none -> 27.6 us  [the longest x4 16.5 us: near(): pl.pallas_call(near_kernel, grid=(channels,), out_shape=jax.ShapeDtypeStr...]
    another operation x8 -> x0, other arithmetic: 15.1 us -> none
    slice x2 -> x0, local copies, waits for them, and re-layouts: 12.2 us -> none  [the longest x1 12.2 us: filter_frames(): framed[:, tap_index:tap_index + spectra_count, :].astype(jnp.float32)]
    unnamed x4 -> x0, local copies, waits for them, and re-layouts: 8.82 us -> none
    ppermute x4 -> x6, starting transfers between devices: 17.6 us -> 11.2 us  [the longest x1 5 us: on_device(): third = lax.ppermute(second, 'blk', BACK)]
    another operation x1 -> x0, local copies, waits for them, and re-layouts: 4.07 us -> none  [channel_table(): jnp.stack([jnp.cos(angles) * factor, -jnp.sin(angles) * factor], axis=2)]
  transfers between devices with their start and end apart: 4 -> 6, of which waited for: 3 -> 3; matrix products, arithmetic and copies ran while one was open for 10% -> 0% of each run, Pallas kernels for 0% -> 13%
where the time goes in v1:
time: 110 us; the launch traced here: 108 us
  blocking collectives  39.2 us (36%)
  waiting for transfers between devices  29.7 us (27%)
  Pallas kernels  27.6 us (25%)
  starting transfers between devices  11.2 us (10%)
    all_to_all x1, blocking collectives, on_device(): lax.all_to_all(pieces, 'grp', split_axis=0, concat_axis=0, tiled=True)  39.2 us
    ppermute x1, waiting for transfers between devices, on_device(): across = lax.ppermute(own, 'blk', SWAP)  20.9 us
    pallas_call x4, Pallas kernels, near(): pl.pallas_call(near_kernel, grid=(channels,), out_shape=jax.ShapeDtypeStr...  16.5 us
    pallas_call x1, Pallas kernels, channelize(): pl.pallas_call(channelize_kernel, out_shape=jax.ShapeDtypeStruct((GROUPS,...  8.83 us
    ppermute x1, waiting for transfers between devices, on_device(): arrived = lax.ppermute(passing, 'blk', RIGHT)  8.27 us
    ppermute x1, starting transfers between devices, on_device(): third = lax.ppermute(second, 'blk', BACK)  5 us
    ppermute x1, starting transfers between devices, on_device(): second = lax.ppermute(own, 'blk', LEFT)  2.77 us
    pallas_call x1, Pallas kernels, far(): pl.pallas_call(far_kernel, grid_spec=pltpu.PrefetchScalarGridSpec(num_sca...  2.21 us
  transfers between devices with their start and end apart: 6, of which 3 were waited for; matrix products, arithmetic and copies ran while one was open for 0% of the time, Pallas kernels for 13%

profile of v1, /device:TPU:48, one launch (start us, length us, event | category | flops | bytes accessed | tf_op | source)
XLA Modules:
  0.0 108.4 jit_solution(3133815892190346585)
XLA Ops:
  0.6 8.8 %channelize.1 = bf16[32,8,8,256]{3,2,1,0:T(8,128)(2,1)} custom-call(bf16[131,8,2048]{2,1,0:T(8,128)(2,1)} %bitcast.10, bf16[512,2048]{1,0:T(8,128)(2,1)} %constant.29.clone.table, f32[4,2048]{1,0:T(4,128)} %constant.30.clone.taps, f32[8,256]{1,0:T(8,128)} %bitcast.11), custom_call_target="tpu_custom_call" | custom-call | tf_op jit(solution)/shard_map/channelize/pallas_call | solution.py:102
  9.5 39.2 %all_to_all.5 = bf16[32,8,8,256]{3,2,1,0:T(8,128)(2,1)S(1)} all-to-all(bf16[32,8,8,256]{3,2,1,0:T(8,128)(2,1)} %channelize.1), channel_id=1, replica_groups=mesh['grp'=32,'blk'=8] {'grp'}, dimensions={0} | all-to-all | bytes 2097152 | tf_op jit(solution)/shard_map/all_to_all | solution.py:207
  48.7 0.1 copy_bitcast_fusion.own.other
  48.8 1.4 %collective-permute-start.2 = (bf16[8,256,256]{2,1,0:T(8,128)(2,1)S(1)}, bf16[8,256,256]{2,1,0:T(8,128)(2,1)S(1)}, u32[]{:S(2)}, u32[]{:S(2)}) collective-permute-start(bf16[8,256,256]{2,1,0:T(8,128)(2,1)S(1)} %copy_bitcast_fusion.own.other), channel_id=1, source_target_pairs={{0,1},{1,0},{2,3},{3,2},{4,5},{5,4},{6,7},{7,6},{8,9},{9,8},{10,11... | collective-permute-start | bytes 3145736 | tf_op jit(solution)/shard_map/ppermute | solution.py:211
  50.1 2.8 %collective-permute-start = (bf16[8,256,256]{2,1,0:T(8,128)(2,1)S(1)}, bf16[8,256,256]{2,1,0:T(8,128)(2,1)S(1)}, u32[]{:S(2)}, u32[]{:S(2)}) collective-permute-start(bf16[8,256,256]{2,1,0:T(8,128)(2,1)S(1)} %copy_bitcast_fusion.own.other), channel_id=1, source_target_pairs={{0,6},{1,7},{2,0},{3,1},{4,2},{5,3},{6,4},{7,5},{8,14},{9,15},{10,... | collective-permute-start | bytes 3145736 | tf_op jit(solution)/shard_map/ppermute | solution.py:210
  52.9 0.1 collective-permute-start.4
  53.0 20.9 %collective-permute-done.2 = bf16[8,256,256]{2,1,0:T(8,128)(2,1)S(1)} collective-permute-done((bf16[8,256,256]{2,1,0:T(8,128)(2,1)S(1)}, bf16[8,256,256]{2,1,0:T(8,128)(2,1)S(1)}, u32[]{:S(2)}, u32[]{:S(2)}) %collective-permute-start.2) | collective-permute-done | bytes 1048608 | tf_op jit(solution)/shard_map/ppermute | solution.py:211
  73.9 0.7 collective-permute-start.3
  74.6 0.6 collective-permute-done.other
  75.2 5.0 %collective-permute-start.1 = (bf16[8,256,256]{2,1,0:T(8,128)(2,1)S(1)}, bf16[8,256,256]{2,1,0:T(8,128)(2,1)S(1)}, u32[]{:S(2)}, u32[]{:S(2)}) collective-permute-start(bf16[8,256,256]{2,1,0:T(8,128)(2,1)S(1)} %collective-permute-done.other), channel_id=1, source_target_pairs={{0,7},{1,0},{2,1},{3,2},{4,3},{5,4},{6,5},{7,6},{8,15},{9,8},{10,9... | collective-permute-start | bytes 3145736 | tf_op jit(solution)/shard_map/ppermute | solution.py:213
  80.2 0.0 collective-permute-done.4
  80.2 1.2 %collective-permute-start.5 = (bf16[4,256,256]{2,1,0:T(8,128)(2,1)S(1)}, bf16[4,256,256]{2,1,0:T(8,128)(2,1)S(1)}, u32[]{:S(2)}, u32[]{:S(2)}) collective-permute-start(bf16[4,256,256]{2,1,0:T(8,128)(2,1)S(1)} %collective-permute-done.4), channel_id=1, source_target_pairs={{0,2},{1,3},{2,4},{3,5},{4,6},{5,7},{6,0},{7,1},{8,10},{9,11},{10,... | collective-permute-start | bytes 1572872 | tf_op jit(solution)/shard_map/ppermute | solution.py:215
  81.4 4.1 %near0.1.rest_0_ = bf16[4,8,2,256,256]{4,3,2,1,0:T(8,128)(2,1)} custom-call(bf16[8,256,256]{2,1,0:T(8,128)(2,1)S(1)} %copy_bitcast_fusion.own.other, bf16[8,256,256]{2,1,0:T(8,128)(2,1)S(1)} %copy_bitcast_fusion.own.other), custom_call_target="tpu_custom_call" | custom-call | flops 536870912 | bytes 4194304 | tf_op jit(solution)/shard_map/near0/pallas_call | solution.py:150
  85.5 8.3 %collective-permute-done.5.other = bf16[4,256,256]{2,1,0:T(8,128)(2,1)S(1)} collective-permute-done((bf16[4,256,256]{2,1,0:T(8,128)(2,1)S(1)}, bf16[4,256,256]{2,1,0:T(8,128)(2,1)S(1)}, u32[]{:S(2)}, u32[]{:S(2)}) %collective-permute-start.5) | collective-permute-done | bytes 524320 | tf_op jit(solution)/shard_map/ppermute | solution.py:215
  93.8 2.2 %far.1 = bf16[4,2,256,256]{3,2,1,0:T(8,128)(2,1)} custom-call(s32[1]{0:T(128)} %bitcast.5.start, bf16[8,256,256]{2,1,0:T(8,128)(2,1)S(1)} %copy_bitcast_fusion.own.other, bf16[4,256,256]{2,1,0:T(8,128)(2,1)S(1)} %collective-permute-done.5.other), custom_call_target="tpu_custom_call" | custom-call | tf_op jit(solution)/shard_map/far/pallas_call | solution.py:173
  96.0 4.1 %near2.1.rest_0_ = bf16[4,8,2,256,256]{4,3,2,1,0:T(8,128)(2,1)} custom-call(bf16[8,256,256]{2,1,0:T(8,128)(2,1)S(1)} %copy_bitcast_fusion.own.other, bf16[8,256,256]{2,1,0:T(8,128)(2,1)S(1)} %collective-permute-done.other, bf16[4,8,2,256,256]{4,3,2,1,0:T(8,128)(2,1)} %near0.1.rest_0_), custom_call_target="tpu_custom_call", output_to_operand_aliasing={{}: (2, {})} | custom-call | flops 536870912 | bytes 4194304 | tf_op jit(solution)/shard_map/near2/pallas_call | solution.py:150
  100.1 0.0 collective-permute-done.3.other
  100.1 4.2 %near1.1.rest_0_ = bf16[4,8,2,256,256]{4,3,2,1,0:T(8,128)(2,1)} custom-call(bf16[8,256,256]{2,1,0:T(8,128)(2,1)S(1)} %copy_bitcast_fusion.own.other, bf16[8,256,256]{2,1,0:T(8,128)(2,1)S(1)} %collective-permute-done.3.other, bf16[4,8,2,256,256]{4,3,2,1,0:T(8,128)(2,1)} %near2.1.rest_0_), custom_call_target="tpu_custom_call", output_to_operand_aliasing={{}: (2, {})} | custom-call | flops 536870912 | bytes 4194304 | tf_op jit(solution)/shard_map/near1/pallas_call | solution.py:150
  104.3 0.0 collective-permute-done.1.other
  104.3 4.1 %near3.1 = bf16[4,8,2,256,256]{4,3,2,1,0:T(8,128)(2,1)} custom-call(bf16[8,256,256]{2,1,0:T(8,128)(2,1)S(1)} %copy_bitcast_fusion.own.other, bf16[8,256,256]{2,1,0:T(8,128)(2,1)S(1)} %collective-permute-done.1.other, bf16[4,8,2,256,256]{4,3,2,1,0:T(8,128)(2,1)} %near1.1.rest_0_), custom_call_target="tpu_custom_call", output_to_operand_aliasing={{}: (2, {})} | custom-call | flops 536870912 | bytes 4194304 | tf_op jit(solution)/shard_map/near3/pallas_call | solution.py:150
  (1 shorter events, 0.0 us)
Async XLA Ops:
  48.8 25.1 %collective-permute-start.2 = (bf16[8,256,256]{2,1,0:T(8,128)(2,1)S(1)}, bf16[8,256,256]{2,1,0:T(8,128)(2,1)S(1)}, u32[]{:S(2)}, u32[]{:S(2)}) collective-permute-start(bf16[8,256,256]{2,1,0:T(8,128)(2,1)S(1)} %copy_bitcast_fusion.own.other), channel_id=1, source_target_pairs={{0,1},{1,0},{2,3},{3,2},{4,5},{5,4},{6,7},{7,6},{8,9},{9,8},{10,11... | collective-permute-start | bytes 3145736 | tf_op jit(solution)/shard_map/ppermute | solution.py:211
  50.1 25.0 %collective-permute-start = (bf16[8,256,256]{2,1,0:T(8,128)(2,1)S(1)}, bf16[8,256,256]{2,1,0:T(8,128)(2,1)S(1)}, u32[]{:S(2)}, u32[]{:S(2)}) collective-permute-start(bf16[8,256,256]{2,1,0:T(8,128)(2,1)S(1)} %copy_bitcast_fusion.own.other), channel_id=1, source_target_pairs={{0,6},{1,7},{2,0},{3,1},{4,2},{5,3},{6,4},{7,5},{8,14},{9,15},{10,... | collective-permute-start | bytes 3145736 | tf_op jit(solution)/shard_map/ppermute | solution.py:210
  52.9 27.2 %collective-permute-start.4 = (bf16[4,256,256]{2,1,0:T(8,128)(2,1)S(1)}, bf16[4,256,256]{2,1,0:T(8,128)(2,1)S(1)}, u32[]{:S(2)}, u32[]{:S(2)}) collective-permute-start(bf16[4,256,256]{2,1,0:T(8,128)(2,1)S(1)} %constant_dynamic-slice_fusion), channel_id=1, source_target_pairs={{0,2},{1,3},{2,4},{3,5},{4,6},{5,7},{6,0},{7,1},{8,10},{9,11},{10,... | collective-permute-start | bytes 1572872 | tf_op jit(solution)/shard_map/ppermute | solution.py:212
  73.9 26.2 %collective-permute-start.3 = (bf16[8,256,256]{2,1,0:T(8,128)(2,1)S(1)}, bf16[8,256,256]{2,1,0:T(8,128)(2,1)S(1)}, u32[]{:S(2)}, u32[]{:S(2)}) collective-permute-start(bf16[8,256,256]{2,1,0:T(8,128)(2,1)S(1)} %collective-permute-done.2), channel_id=1, source_target_pairs={{0,0},{1,7},{2,2},{3,1},{4,4},{5,3},{6,6},{7,5},{8,8},{9,15},{10,1... | collective-permute-start | bytes 3145736 | tf_op jit(solution)/shard_map/ppermute | solution.py:214
  75.2 29.1 %collective-permute-start.1 = (bf16[8,256,256]{2,1,0:T(8,128)(2,1)S(1)}, bf16[8,256,256]{2,1,0:T(8,128)(2,1)S(1)}, u32[]{:S(2)}, u32[]{:S(2)}) collective-permute-start(bf16[8,256,256]{2,1,0:T(8,128)(2,1)S(1)} %collective-permute-done.other), channel_id=1, source_target_pairs={{0,7},{1,0},{2,1},{3,2},{4,3},{5,4},{6,5},{7,6},{8,15},{9,8},{10,9... | collective-permute-start | bytes 3145736 | tf_op jit(solution)/shard_map/ppermute | solution.py:213
  80.2 13.6 %collective-permute-start.5 = (bf16[4,256,256]{2,1,0:T(8,128)(2,1)S(1)}, bf16[4,256,256]{2,1,0:T(8,128)(2,1)S(1)}, u32[]{:S(2)}, u32[]{:S(2)}) collective-permute-start(bf16[4,256,256]{2,1,0:T(8,128)(2,1)S(1)} %collective-permute-done.4), channel_id=1, source_target_pairs={{0,2},{1,3},{2,4},{3,5},{4,6},{5,7},{6,0},{7,1},{8,10},{9,11},{10,... | collective-permute-start | bytes 1572872 | tf_op jit(solution)/shard_map/ppermute | solution.py:215

commit v2 on v1

v2 whole, which is shorter than its diff:
```python
import math

import jax
import jax.numpy as jnp
import numpy as np
from jax import lax
from jax.experimental import pallas as pl
from jax.experimental.pallas import tpu as pltpu
from jax.sharding import PartitionSpec as P

TAPS = 4
BAND = 256
SPEC = 128
FRAME = 2048
GROUPS = 32
PER = 8
SHARE = 8
ROWS = GROUPS * 2 * PER
LANES = 2 * SPEC
MIB = 1024 * 1024


def prototype_taps():
    position = (np.arange(TAPS * FRAME, dtype=np.float64) + 0.5) / (TAPS * FRAME)
    window = 0.5 - 0.5 * np.cos(2.0 * np.pi * position)
    return (np.sinc(TAPS * (position - 0.5)) * window).reshape(TAPS, FRAME).astype(np.float32)


def channel_table():
    phase = (np.arange(FRAME)[None, :] * (BAND + np.arange(GROUPS * PER))[:, None]) % FRAME
    angles = phase * (2.0 * np.pi / FRAME)
    factor = 0.25 / math.sqrt(FRAME)
    parts = np.stack([np.cos(angles) * factor, -np.sin(angles) * factor], axis=0)
    table = parts.reshape(2, GROUPS, PER, FRAME).transpose(1, 0, 2, 3).reshape(ROWS, FRAME)
    return table.astype(np.float32).astype(jnp.bfloat16).reshape(GROUPS, 2 * PER, FRAME)


def constant_tables():
    rest = prototype_taps()
    parts = []
    for _ in range(3):
        part = rest.astype(jnp.bfloat16)
        parts.append(part)
        rest = rest - part.astype(np.float32)
    parts.append(np.zeros_like(parts[0]))
    return np.concatenate([channel_table(), np.concatenate(parts, axis=0)[None]], axis=0)


COL = 128
STEP = 512
STEPS = FRAME // STEP
WIDTH = GROUPS * SHARE
VMEM = pltpu.VMEM


def whole_vmem():
    return pl.BlockSpec(memory_space=VMEM)


def far_start():
    half_count = lax.axis_size("blk") // 2
    return lax.axis_index("blk") // half_count * (PER // 2)


def channelize_kernel(samples, table, gains, out, held, rows, frames, total, turned, parts_of_taps, taps, sem_in, sem_table, sem_taps):
    def columns(step):
        return pl.ds(pl.multiple_of(step * STEP, STEP), STEP)

    def sample_copy(step):
        lanes = columns(step)
        return pltpu.make_async_copy(samples.at[:, :, lanes], held.at[:, :, lanes], sem_in.at[step])

    table_copy = pltpu.make_async_copy(table.at[pl.ds(0, GROUPS)], rows, sem_table)
    taps_copy = pltpu.make_async_copy(table.at[GROUPS], parts_of_taps, sem_taps)
    taps_copy.start()
    sample_copy(0).start()
    sample_copy(1).start()
    table_copy.start()
    for step in range(2, STEPS):
        sample_copy(step).start()
    taps_copy.wait()
    split = parts_of_taps[...].astype(jnp.float32)
    taps[...] = split[:TAPS] + (split[TAPS : 2 * TAPS] + split[2 * TAPS : 3 * TAPS])

    def filter_step(step, slot):
        for b in range(STEP // COL):
            lanes = pl.ds(pl.multiple_of(step * STEP + b * COL, COL), COL)
            weights = [jnp.broadcast_to(taps[t : t + 1, lanes], (SHARE, COL)) for t in range(TAPS)]
            window = [held[t, :, lanes].astype(jnp.float32) for t in range(TAPS - 1)]
            for s in range(SPEC):
                window.append(held[s + TAPS - 1, :, lanes].astype(jnp.float32))
                value = weights[0] * window[0]
                for t in range(1, TAPS):
                    value = value + weights[t] * window[t]
                frames[slot, b, s * SHARE : (s + 1) * SHARE, :] = value
                window = window[1:]

    def transform_step(step, slot, first=False):
        chosen = []
        for n in range(SHARE):
            blocks = [frames[slot, b, pl.ds(n, SPEC, stride=SHARE), :] for b in range(STEP // COL)]
            chosen.append(jnp.concatenate([block.astype(jnp.bfloat16) for block in blocks], axis=1))
        product = lax.dot_general(
            rows[:, :, columns(step)].reshape(ROWS, STEP),
            jnp.concatenate(chosen, axis=0),
            (((1,), (1,)), ((), ())),
            preferred_element_type=jnp.float32,
        )
        total[...] = product if first else total[...] + product

    sample_copy(0).wait()
    filter_step(0, 0)
    table_copy.wait()
    sample_copy(1).wait()
    filter_step(1, 1)
    transform_step(0, 0, True)

    def two_steps(j, carry):
        for k in range(2):
            step = 2 * j + 2 + k
            sample_copy(step).wait()
            filter_step(step, k)
            transform_step(step - 1, 1 - k)
        return carry

    lax.fori_loop(0, STEPS // 2 - 1, two_steps, 0)
    transform_step(STEPS - 1, 1)
    scale = jnp.transpose(gains[...]).reshape(GROUPS, PER, SHARE)
    for n in range(SHARE):
        factor = scale[:, :, n : n + 1].reshape(GROUPS, 1, PER, 1)
        mine = total[:, n * SPEC : (n + 1) * SPEC].reshape(GROUPS, 2, PER, SPEC) * factor
        turned[pl.ds(n, ROWS, stride=SHARE), :] = mine.reshape(ROWS, SPEC)
    whole = turned[...].reshape(GROUPS, 2, PER, SHARE, SPEC)
    for r in range(2):
        out[:, :, :, r * SPEC : (r + 1) * SPEC] = whole[:, r].astype(jnp.bfloat16)


def channelize(samples, gains):
    by_frame = jnp.transpose(samples.reshape(SHARE, SPEC + TAPS - 1, FRAME), (1, 0, 2))
    return pl.pallas_call(
        channelize_kernel,
        out_shape=jax.ShapeDtypeStruct((GROUPS, PER, SHARE, LANES), jnp.bfloat16),
        in_specs=[
            pl.BlockSpec(memory_space=pltpu.HBM),
            pl.BlockSpec(memory_space=pltpu.HBM),
            whole_vmem(),
        ],
        out_specs=whole_vmem(),
        scratch_shapes=[
            VMEM((SPEC + TAPS - 1, SHARE, FRAME), jnp.bfloat16),
            VMEM((GROUPS, 2 * PER, FRAME), jnp.bfloat16),
            VMEM((2, STEP // COL, SPEC * SHARE, COL), jnp.float32),
            VMEM((ROWS, SHARE * SPEC), jnp.float32),
            VMEM((ROWS * SHARE, SPEC), jnp.float32),
            VMEM((4 * TAPS, FRAME), jnp.bfloat16),
            VMEM((TAPS, FRAME), jnp.float32),
            pltpu.SemaphoreType.DMA((STEPS,)),
            pltpu.SemaphoreType.DMA,
            pltpu.SemaphoreType.DMA,
        ],
        compiler_params=pltpu.CompilerParams(vmem_limit_bytes=52 * MIB),
        name="channelize",
    )(by_frame, constant_tables(), gains)


def own_kernel(pieces, low, high, outgoing):
    half = PER // 2
    for g in range(GROUPS):
        rows = slice(g * SHARE, (g + 1) * SHARE)
        low[:, rows, :] = pieces[g, :half]
        high[:, rows, :] = pieces[g, half:]

    @pl.when(far_start() == 0)
    def _():
        outgoing[...] = high[...]

    @pl.when(far_start() != 0)
    def _():
        outgoing[...] = low[...]


def own_halves(pieces):
    half = jax.ShapeDtypeStruct((PER // 2, WIDTH, LANES), jnp.bfloat16)
    return pl.pallas_call(
        own_kernel,
        out_shape=(half,) * 3,
        in_specs=[whole_vmem()],
        out_specs=(whole_vmem(),) * 3,
        compiler_params=pltpu.CompilerParams(vmem_limit_bytes=16 * MIB),
        name="own_halves",
    )(pieces)


def correlate_one(mine, other):
    crossed = jnp.concatenate([mine[:, SPEC:], -mine[:, :SPEC]], axis=1)
    contract = (((1,), (1,)), ((), ()))
    real = lax.dot_general(mine, other, contract, preferred_element_type=jnp.float32)
    imag = lax.dot_general(crossed, other, contract, preferred_element_type=jnp.float32)
    return (real * (1.0 / SPEC)).astype(jnp.bfloat16), (imag * (1.0 / SPEC)).astype(jnp.bfloat16)


def correlate(own, items, before, half_count, arrived=None):
    others = [other for _, _, other in items if other is not None]
    has_far = arrived is not None
    half, width, lanes = own[0].shape

    def kernel(*refs):
        refs = list(refs)
        mine = (refs.pop(0), refs.pop(0))
        sources = [mine[part] if other is None else refs.pop(0) for _, part, other in items]
        arrived = refs.pop(0) if has_far else None
        if before is not None:
            refs.pop(0)
        out = refs.pop(0)
        out_far = refs.pop(0) if has_far else None
        results, sems = refs[:2]
        copies = []
        for j, (offset, part, _) in enumerate(items):
            for c in range(half):
                real, imag = correlate_one(mine[part][c], sources[j][c])
                results[j, c, 0] = real
                results[j, c, 1] = imag
                copy = pltpu.make_async_copy(
                    results.at[j, c], out.at[offset, part * half + c], sems.at[j, c]
                )
                copy.start()
                copies.append(copy)
        if has_far:
            far_results, far_sems = refs[2:]
            low = far_start() == 0
            for c in range(half):
                real, imag = correlate_one(jnp.where(low, mine[0][c], mine[1][c]), arrived[c])
                far_results[c, 0] = real
                far_results[c, 1] = imag
                copy = pltpu.make_async_copy(far_results.at[c], out_far.at[c], far_sems.at[c])
                copy.start()
                copies.append(copy)
        for copy in copies:
            copy.wait()

    near_shape = jax.ShapeDtypeStruct((half_count, PER, 2, width, width), jnp.bfloat16)
    far_shape = jax.ShapeDtypeStruct((half, 2, width, width), jnp.bfloat16)
    operands = [*own, *others] + ([arrived] if has_far else [])
    specs = [whole_vmem()] * len(operands)
    aliases = {}
    if before is not None:
        aliases = {len(operands): 0}
        operands.append(before)
        specs.append(pl.BlockSpec(memory_space=pl.ANY))
    count = len(items)
    scratch = [
        VMEM((count, half, 2, width, width), jnp.bfloat16),
        pltpu.SemaphoreType.DMA((count, half)),
    ]
    if has_far:
        scratch += [VMEM((half, 2, width, width), jnp.bfloat16), pltpu.SemaphoreType.DMA((half,))]
    channels = (count + has_far) * half
    return pl.pallas_call(
        kernel,
        out_shape=(near_shape, far_shape) if has_far else near_shape,
        in_specs=specs,
        out_specs=(pl.BlockSpec(memory_space=pl.ANY),) * 2 if has_far else pl.BlockSpec(memory_space=pl.ANY),
        input_output_aliases=aliases,
        scratch_shapes=scratch,
        cost_estimate=pl.CostEstimate(
            flops=channels * 4 * width * width * lanes,
            bytes_accessed=channels * 4 * width * width,
            transcendentals=0,
        ),
        compiler_params=pltpu.CompilerParams(vmem_limit_bytes=24 * MIB),
        name="correlate_" + "_".join(str(offset) for offset, _, _ in items),
    )(*operands)


def blk_route(step):
    return [(2 * x + l, step(x, l)) for x in range(4) for l in range(2)]


LEFT = blk_route(lambda x, l: 2 * ((x - 1) % 4) + l)
RIGHT = blk_route(lambda x, l: 2 * ((x + 1) % 4) + l)
SWAP = blk_route(lambda x, l: 2 * x + 1 - l)
BACK = blk_route(lambda x, l: (2 * x + l - 1) % 8)
LEFT_ODD = blk_route(lambda x, l: 2 * ((x - l) % 4) + l)


def send(block, axis, route):
    return lax.ppermute(block, axis, route)


def all_arrived(*arrays):
    return lax.optimization_barrier(arrays)


def on_device(samples, input_gains):
    half_count = lax.axis_size("blk") // 2
    pieces = channelize(samples[0], input_gains[0])
    pieces = lax.all_to_all(pieces, "grp", split_axis=0, concat_axis=0, tiled=True)
    *own, outgoing = own_halves(pieces)
    across, second, first, third = [], [], [], []
    for part in range(2):
        second.append(send(own[part], "blk", LEFT))
        across.append(send(own[part], "blk", SWAP))
    passing = send(outgoing, "blk", RIGHT)
    for part in range(2):
        across[part], second[part] = all_arrived(across[part], second[part])
        first.append(send(across[part], "blk", LEFT_ODD))
        third.append(send(second[part], "blk", BACK))
    arrived = send(passing, "blk", RIGHT)
    vis_near = correlate(own, [(0, 0, None), (0, 1, None)], None, half_count)
    vis_near = correlate(own, [(2, 0, second[0]), (2, 1, second[1])], vis_near, half_count)
    vis_near = correlate(own, [(1, 0, first[0]), (3, 0, third[0])], vis_near, half_count)
    last = [(1, 1, first[1]), (3, 1, third[1])]
    vis_near, vis_far = correlate(own, last, vis_near, half_count, arrived)
    return (vis_near, vis_far)


def solution(mesh):
    return jax.shard_map(
        on_device,
        mesh=mesh,
        in_specs=(P("blk", "grp", None), P("blk", "grp", None)),
        out_specs=(P(None, "grp", None, "blk", None), P("grp", None, "blk", None)),
        check_vma=False,
    )
```

time: 110 us -> 101 us (0.918)
  the two profiles are of different devices: /device:TPU:48 before, /device:TPU:30 now
where the time goes in v2:
time: 101 us
  blocking collectives  40.3 us (40%)
  waiting for transfers between devices  28.5 us (28%)
  starting transfers between devices  16 us (16%)
  Pallas kernels  14.4 us (14%)
    all_to_all x1, blocking collectives, on_device(): lax.all_to_all(pieces, 'grp', split_axis=0, concat_axis=0, tiled=True)  40.3 us
    ppermute x10, waiting for transfers between devices, send(): return lax.ppermute(block, axis, route)  28.5 us
    ppermute x10, starting transfers between devices, send(): return lax.ppermute(block, axis, route)  16 us
    pallas_call x1, Pallas kernels, channelize(): pl.pallas_call(channelize_kernel, out_shape=jax.ShapeDtypeStruct((GROUPS,...  7.3 us
    pallas_call x4, Pallas kernels, correlate(): pl.pallas_call(kernel, out_shape=(near_shape, far_shape) if has_far else...  6.95 us
  transfers between devices with their start and end apart: 10, of which 6 were waited for; matrix products, arithmetic and copies ran while one was open for 0% of the time, Pallas kernels for 5%

profile of v2, /device:TPU:30, one launch (start us, length us, event | category | flops | bytes accessed | tf_op | source)
XLA Modules:
  0.0 100.7 jit_solution(3366182947219887783)
XLA Ops:
  0.6 0.7 copy-done
  1.3 7.3 %channelize.1 = bf16[32,8,8,256]{3,2,1,0:T(8,128)(2,1)S(1)} custom-call(bf16[131,8,2048]{2,1,0:T(8,128)(2,1)} %bitcast.5, bf16[33,16,2048]{2,1,0:T(8,128)(2,1)} %constant.2.clone.table, f32[8,256]{1,0:T(8,128)S(1)} %bitcast.4), custom_call_target="tpu_custom_call" | custom-call | tf_op jit(solution)/shard_map/channelize/pallas_call | solution.py:140
  8.6 40.3 %all_to_all.5.pieces = bf16[32,8,8,256]{3,2,1,0:T(8,128)(2,1)S(1)} all-to-all(bf16[32,8,8,256]{3,2,1,0:T(8,128)(2,1)S(1)} %channelize.1), channel_id=1, replica_groups=mesh['grp'=32,'blk'=8] {'grp'}, dimensions={0} | all-to-all | bytes 2097152 | tf_op jit(solution)/shard_map/all_to_all | solution.py:297
  49.0 0.1 own_halves.1
  49.1 0.8 collective-permute-start.6
  49.9 0.8 collective-permute-start.7
  50.7 1.3 %collective-permute-start = (bf16[4,256,256]{2,1,0:T(8,128)(2,1)S(1)}, bf16[4,256,256]{2,1,0:T(8,128)(2,1)S(1)}, u32[]{:S(2)}, u32[]{:S(2)}) collective-permute-start(bf16[4,256,256]{2,1,0:T(8,128)(2,1)S(1)} %get-tuple-element.10.refs_1_), channel_id=1, source_target_pairs={{0,1},{1,0},{2,3},{3,2},{4,5},{5,4},{6,7},{7,6},{8,9},{9,8},{10,11... | collective-permute-start | bytes 1572872 | tf_op jit(solution)/shard_map/ppermute | solution.py:287
  52.0 0.5 collective-permute-start.1
  52.6 2.7 %collective-permute-start.4 = (bf16[4,256,256]{2,1,0:T(8,128)(2,1)S(1)}, bf16[4,256,256]{2,1,0:T(8,128)(2,1)S(1)}, u32[]{:S(2)}, u32[]{:S(2)}) collective-permute-start(bf16[4,256,256]{2,1,0:T(8,128)(2,1)S(1)} %get-tuple-element.13), channel_id=1, source_target_pairs={{0,2},{1,3},{2,4},{3,5},{4,6},{5,7},{6,0},{7,1},{8,10},{9,11},{10,... | collective-permute-start | bytes 1572872 | tf_op jit(solution)/shard_map/ppermute | solution.py:287
  55.3 8.8 %collective-permute-done.6 = bf16[4,256,256]{2,1,0:T(8,128)(2,1)S(1)} collective-permute-done((bf16[4,256,256]{2,1,0:T(8,128)(2,1)S(1)}, bf16[4,256,256]{2,1,0:T(8,128)(2,1)S(1)}, u32[]{:S(2)}, u32[]{:S(2)}) %collective-permute-start.6) | collective-permute-done | bytes 524320 | tf_op jit(solution)/shard_map/ppermute | solution.py:287
  64.0 2.0 %collective-permute-done.7.refs_2_ = bf16[4,256,256]{2,1,0:T(8,128)(2,1)S(1)} collective-permute-done((bf16[4,256,256]{2,1,0:T(8,128)(2,1)S(1)}, bf16[4,256,256]{2,1,0:T(8,128)(2,1)S(1)}, u32[]{:S(2)}, u32[]{:S(2)}) %collective-permute-start.7) | collective-permute-done | bytes 524320 | tf_op jit(solution)/shard_map/ppermute | solution.py:287
  66.0 1.3 %collective-permute-start.9 = (bf16[4,256,256]{2,1,0:T(8,128)(2,1)S(1)}, bf16[4,256,256]{2,1,0:T(8,128)(2,1)S(1)}, u32[]{:S(2)}, u32[]{:S(2)}) collective-permute-start(bf16[4,256,256]{2,1,0:T(8,128)(2,1)S(1)} %collective-permute-done.7.refs_2_), channel_id=1, source_target_pairs={{0,7},{1,0},{2,1},{3,2},{4,3},{5,4},{6,5},{7,6},{8,15},{9,8},{10,9... | collective-permute-start | bytes 1572872 | tf_op jit(solution)/shard_map/ppermute | solution.py:287
  67.3 1.9 %collective-permute-start.8 = (bf16[4,256,256]{2,1,0:T(8,128)(2,1)S(1)}, bf16[4,256,256]{2,1,0:T(8,128)(2,1)S(1)}, u32[]{:S(2)}, u32[]{:S(2)}) collective-permute-start(bf16[4,256,256]{2,1,0:T(8,128)(2,1)S(1)} %collective-permute-done.6), channel_id=1, source_target_pairs={{0,0},{1,7},{2,2},{3,1},{4,4},{5,3},{6,6},{7,5},{8,8},{9,15},{10,1... | collective-permute-start | bytes 1572872 | tf_op jit(solution)/shard_map/ppermute | solution.py:287
  69.2 4.5 %collective-permute-done = bf16[4,256,256]{2,1,0:T(8,128)(2,1)S(1)} collective-permute-done((bf16[4,256,256]{2,1,0:T(8,128)(2,1)S(1)}, bf16[4,256,256]{2,1,0:T(8,128)(2,1)S(1)}, u32[]{:S(2)}, u32[]{:S(2)}) %collective-permute-start) | collective-permute-done | bytes 524320 | tf_op jit(solution)/shard_map/ppermute | solution.py:287
  73.7 3.5 %collective-permute-done.1.refs_3_ = bf16[4,256,256]{2,1,0:T(8,128)(2,1)S(1)} collective-permute-done((bf16[4,256,256]{2,1,0:T(8,128)(2,1)S(1)}, bf16[4,256,256]{2,1,0:T(8,128)(2,1)S(1)}, u32[]{:S(2)}, u32[]{:S(2)}) %collective-permute-start.1) | collective-permute-done | bytes 524320 | tf_op jit(solution)/shard_map/ppermute | solution.py:287
  77.2 1.3 %collective-permute-start.3 = (bf16[4,256,256]{2,1,0:T(8,128)(2,1)S(1)}, bf16[4,256,256]{2,1,0:T(8,128)(2,1)S(1)}, u32[]{:S(2)}, u32[]{:S(2)}) collective-permute-start(bf16[4,256,256]{2,1,0:T(8,128)(2,1)S(1)} %collective-permute-done.1.refs_3_), channel_id=1, source_target_pairs={{0,7},{1,0},{2,1},{3,2},{4,3},{5,4},{6,5},{7,6},{8,15},{9,8},{10,9... | collective-permute-start | bytes 1572872 | tf_op jit(solution)/shard_map/ppermute | solution.py:287
  78.5 1.9 %collective-permute-start.2 = (bf16[4,256,256]{2,1,0:T(8,128)(2,1)S(1)}, bf16[4,256,256]{2,1,0:T(8,128)(2,1)S(1)}, u32[]{:S(2)}, u32[]{:S(2)}) collective-permute-start(bf16[4,256,256]{2,1,0:T(8,128)(2,1)S(1)} %collective-permute-done), channel_id=1, source_target_pairs={{0,0},{1,7},{2,2},{3,1},{4,4},{5,3},{6,6},{7,5},{8,8},{9,15},{10,1... | collective-permute-start | bytes 1572872 | tf_op jit(solution)/shard_map/ppermute | solution.py:287
  80.4 3.5 %collective-permute-start.5 = (bf16[4,256,256]{2,1,0:T(8,128)(2,1)S(1)}, bf16[4,256,256]{2,1,0:T(8,128)(2,1)S(1)}, u32[]{:S(2)}, u32[]{:S(2)}) collective-permute-start(bf16[4,256,256]{2,1,0:T(8,128)(2,1)S(1)} %collective-permute-done.4), channel_id=1, source_target_pairs={{0,2},{1,3},{2,4},{3,5},{4,6},{5,7},{6,0},{7,1},{8,10},{9,11},{10,... | collective-permute-start | bytes 1572872 | tf_op jit(solution)/shard_map/ppermute | solution.py:287
  83.9 1.6 %correlate_0_0.1.refs_4_ = bf16[4,8,2,256,256]{4,3,2,1,0:T(8,128)(2,1)} custom-call(bf16[4,256,256]{2,1,0:T(8,128)(2,1)S(1)} %get-tuple-element.9.refs_0_, bf16[4,256,256]{2,1,0:T(8,128)(2,1)S(1)} %get-tuple-element.10.refs_1_), custom_call_target="tpu_custom_call" | custom-call | flops 536870912 | bytes 2097152 | tf_op jit(solution)/shard_map/correlate_0_0/pallas_call | solution.py:258
  85.6 1.6 %correlate_2_2.1.refs_4_ = bf16[4,8,2,256,256]{4,3,2,1,0:T(8,128)(2,1)} custom-call(bf16[4,256,256]{2,1,0:T(8,128)(2,1)S(1)} %get-tuple-element.9.refs_0_, bf16[4,256,256]{2,1,0:T(8,128)(2,1)S(1)} %get-tuple-element.10.refs_1_, bf16[4,256,256]{2,1,0:T(8,128)(2,1)S(1)} %collective-permute-done.7.refs_2_, ...), custom_call_target="tpu_custom_call", output_to_operand_aliasing={{}: (4, {})} | custom-call | flops 536870912 | bytes 2097152 | tf_op jit(solution)/shard_map/correlate_2_2/pallas_call | solution.py:258
  87.2 2.0 %collective-permute-done.9.refs_3_ = bf16[4,256,256]{2,1,0:T(8,128)(2,1)S(1)} collective-permute-done((bf16[4,256,256]{2,1,0:T(8,128)(2,1)S(1)}, bf16[4,256,256]{2,1,0:T(8,128)(2,1)S(1)}, u32[]{:S(2)}, u32[]{:S(2)}) %collective-permute-start.9) | collective-permute-done | bytes 524320 | tf_op jit(solution)/shard_map/ppermute | solution.py:287
  89.2 1.6 %correlate_1_3.2.refs_5_ = bf16[4,8,2,256,256]{4,3,2,1,0:T(8,128)(2,1)} custom-call(bf16[4,256,256]{2,1,0:T(8,128)(2,1)S(1)} %get-tuple-element.9.refs_0_, bf16[4,256,256]{2,1,0:T(8,128)(2,1)S(1)} %get-tuple-element.10.refs_1_, bf16[4,256,256]{2,1,0:T(8,128)(2,1)S(1)} %collective-permute-done.8.refs_2_, ...), custom_call_target="tpu_custom_call", output_to_operand_aliasing={{}: (4, {})} | custom-call | flops 536870912 | bytes 2097152 | tf_op jit(solution)/shard_map/correlate_1_3/pallas_call | solution.py:258
  90.8 7.7 %collective-permute-done.3.refs_3_ = bf16[4,256,256]{2,1,0:T(8,128)(2,1)S(1)} collective-permute-done((bf16[4,256,256]{2,1,0:T(8,128)(2,1)S(1)}, bf16[4,256,256]{2,1,0:T(8,128)(2,1)S(1)}, u32[]{:S(2)}, u32[]{:S(2)}) %collective-permute-start.3) | collective-permute-done | bytes 524320 | tf_op jit(solution)/shard_map/ppermute | solution.py:287
  98.6 2.0 %correlate_1_3.3 = (bf16[4,8,2,256,256]{4,3,2,1,0:T(8,128)(2,1)}, bf16[4,2,256,256]{3,2,1,0:T(8,128)(2,1)}) custom-call(bf16[4,256,256]{2,1,0:T(8,128)(2,1)S(1)} %get-tuple-element.9.refs_0_, bf16[4,256,256]{2,1,0:T(8,128)(2,1)S(1)} %get-tuple-element.10.refs_1_, ...), custom_call_target="tpu_custom_call", output_to_operand_aliasing={{0}: (5, {})} | custom-call | flops 805306368 | bytes 3145728 | tf_op jit(solution)/shard_map/correlate_1_3/pallas_call | solution.py:258
  (5 shorter events, 0.0 us)
Async XLA Ops:
  0.6 0.7 copy-start
  49.1 14.9 %collective-permute-start.6 = (bf16[4,256,256]{2,1,0:T(8,128)(2,1)S(1)}, bf16[4,256,256]{2,1,0:T(8,128)(2,1)S(1)}, u32[]{:S(2)}, u32[]{:S(2)}) collective-permute-start(bf16[4,256,256]{2,1,0:T(8,128)(2,1)S(1)} %get-tuple-element.9.refs_0_), channel_id=1, source_target_pairs={{0,1},{1,0},{2,3},{3,2},{4,5},{5,4},{6,7},{7,6},{8,9},{9,8},{10,11... | collective-permute-start | bytes 1572872 | tf_op jit(solution)/shard_map/ppermute | solution.py:287
  49.9 16.1 %collective-permute-start.7 = (bf16[4,256,256]{2,1,0:T(8,128)(2,1)S(1)}, bf16[4,256,256]{2,1,0:T(8,128)(2,1)S(1)}, u32[]{:S(2)}, u32[]{:S(2)}) collective-permute-start(bf16[4,256,256]{2,1,0:T(8,128)(2,1)S(1)} %get-tuple-element.9.refs_0_), channel_id=1, source_target_pairs={{0,6},{1,7},{2,0},{3,1},{4,2},{5,3},{6,4},{7,5},{8,14},{9,15},{10,... | collective-permute-start | bytes 1572872 | tf_op jit(solution)/shard_map/ppermute | solution.py:287
  50.7 23.0 %collective-permute-start = (bf16[4,256,256]{2,1,0:T(8,128)(2,1)S(1)}, bf16[4,256,256]{2,1,0:T(8,128)(2,1)S(1)}, u32[]{:S(2)}, u32[]{:S(2)}) collective-permute-start(bf16[4,256,256]{2,1,0:T(8,128)(2,1)S(1)} %get-tuple-element.10.refs_1_), channel_id=1, source_target_pairs={{0,1},{1,0},{2,3},{3,2},{4,5},{5,4},{6,7},{7,6},{8,9},{9,8},{10,11... | collective-permute-start | bytes 1572872 | tf_op jit(solution)/shard_map/ppermute | solution.py:287
  52.0 25.2 %collective-permute-start.1 = (bf16[4,256,256]{2,1,0:T(8,128)(2,1)S(1)}, bf16[4,256,256]{2,1,0:T(8,128)(2,1)S(1)}, u32[]{:S(2)}, u32[]{:S(2)}) collective-permute-start(bf16[4,256,256]{2,1,0:T(8,128)(2,1)S(1)} %get-tuple-element.10.refs_1_), channel_id=1, source_target_pairs={{0,6},{1,7},{2,0},{3,1},{4,2},{5,3},{6,4},{7,5},{8,14},{9,15},{10,... | collective-permute-start | bytes 1572872 | tf_op jit(solution)/shard_map/ppermute | solution.py:287
  52.6 27.9 %collective-permute-start.4 = (bf16[4,256,256]{2,1,0:T(8,128)(2,1)S(1)}, bf16[4,256,256]{2,1,0:T(8,128)(2,1)S(1)}, u32[]{:S(2)}, u32[]{:S(2)}) collective-permute-start(bf16[4,256,256]{2,1,0:T(8,128)(2,1)S(1)} %get-tuple-element.13), channel_id=1, source_target_pairs={{0,2},{1,3},{2,4},{3,5},{4,6},{5,7},{6,0},{7,1},{8,10},{9,11},{10,... | collective-permute-start | bytes 1572872 | tf_op jit(solution)/shard_map/ppermute | solution.py:287
  66.0 23.2 %collective-permute-start.9 = (bf16[4,256,256]{2,1,0:T(8,128)(2,1)S(1)}, bf16[4,256,256]{2,1,0:T(8,128)(2,1)S(1)}, u32[]{:S(2)}, u32[]{:S(2)}) collective-permute-start(bf16[4,256,256]{2,1,0:T(8,128)(2,1)S(1)} %collective-permute-done.7.refs_2_), channel_id=1, source_target_pairs={{0,7},{1,0},{2,1},{3,2},{4,3},{5,4},{6,5},{7,6},{8,15},{9,8},{10,9... | collective-permute-start | bytes 1572872 | tf_op jit(solution)/shard_map/ppermute | solution.py:287
  67.3 21.9 %collective-permute-start.8 = (bf16[4,256,256]{2,1,0:T(8,128)(2,1)S(1)}, bf16[4,256,256]{2,1,0:T(8,128)(2,1)S(1)}, u32[]{:S(2)}, u32[]{:S(2)}) collective-permute-start(bf16[4,256,256]{2,1,0:T(8,128)(2,1)S(1)} %collective-permute-done.6), channel_id=1, source_target_pairs={{0,0},{1,7},{2,2},{3,1},{4,4},{5,3},{6,6},{7,5},{8,8},{9,15},{10,1... | collective-permute-start | bytes 1572872 | tf_op jit(solution)/shard_map/ppermute | solution.py:287
  77.2 21.3 %collective-permute-start.3 = (bf16[4,256,256]{2,1,0:T(8,128)(2,1)S(1)}, bf16[4,256,256]{2,1,0:T(8,128)(2,1)S(1)}, u32[]{:S(2)}, u32[]{:S(2)}) collective-permute-start(bf16[4,256,256]{2,1,0:T(8,128)(2,1)S(1)} %collective-permute-done.1.refs_3_), channel_id=1, source_target_pairs={{0,7},{1,0},{2,1},{3,2},{4,3},{5,4},{6,5},{7,6},{8,15},{9,8},{10,9... | collective-permute-start | bytes 1572872 | tf_op jit(solution)/shard_map/ppermute | solution.py:287
  78.5 20.1 %collective-permute-start.2 = (bf16[4,256,256]{2,1,0:T(8,128)(2,1)S(1)}, bf16[4,256,256]{2,1,0:T(8,128)(2,1)S(1)}, u32[]{:S(2)}, u32[]{:S(2)}) collective-permute-start(bf16[4,256,256]{2,1,0:T(8,128)(2,1)S(1)} %collective-permute-done), channel_id=1, source_target_pairs={{0,0},{1,7},{2,2},{3,1},{4,4},{5,3},{6,6},{7,5},{8,8},{9,15},{10,1... | collective-permute-start | bytes 1572872 | tf_op jit(solution)/shard_map/ppermute | solution.py:287
  80.4 18.1 %collective-permute-start.5 = (bf16[4,256,256]{2,1,0:T(8,128)(2,1)S(1)}, bf16[4,256,256]{2,1,0:T(8,128)(2,1)S(1)}, u32[]{:S(2)}, u32[]{:S(2)}) collective-permute-start(bf16[4,256,256]{2,1,0:T(8,128)(2,1)S(1)} %collective-permute-done.4), channel_id=1, source_target_pairs={{0,2},{1,3},{2,4},{3,5},{4,6},{5,7},{6,0},{7,1},{8,10},{9,11},{10,... | collective-permute-start | bytes 1572872 | tf_op jit(solution)/shard_map/ppermute | solution.py:287

commit v3 on v2

--- a/solution.py
+++ b/solution.py
@@ -57,9 +57,16 @@
     return pl.BlockSpec(memory_space=VMEM)
 
 
-def far_start():
-    half_count = lax.axis_size("blk") // 2
-    return lax.axis_index("blk") // half_count * (PER // 2)
+CHUNKS = PER // 2
+
+
+def blk_place():
+    index = lax.axis_index("blk")
+    return index // 2, index % 2
+
+
+def far_half(x):
+    return x // 2
 
 
 def channelize_kernel(samples, table, gains, out, held, rows, frames, total, turned, parts_of_taps, taps, sem_in, sem_table, sem_taps):
@@ -163,32 +170,64 @@
     )(by_frame, constant_tables(), gains)
 
 
-def own_kernel(pieces, low, high, outgoing):
-    half = PER // 2
+def small_kernel(kernel, name, out_shape, *operands):
+    return pl.pallas_call(
+        kernel,
+        out_shape=out_shape,
+        in_specs=[whole_vmem()] * len(operands),
+        out_specs=jax.tree.map(lambda _: whole_vmem(), out_shape),
+        compiler_params=pltpu.CompilerParams(vmem_limit_bytes=16 * MIB),
+        name=name,
+    )(*operands)
+
+
+def blocks(*lead):
+    return jax.ShapeDtypeStruct((*lead, WIDTH, LANES), jnp.bfloat16)
+
+
+def own_kernel(pieces, *outs):
+    chunks, outgoing = outs[:CHUNKS], outs[CHUNKS]
     for g in range(GROUPS):
         rows = slice(g * SHARE, (g + 1) * SHARE)
-        low[:, rows, :] = pieces[g, :half]
-        high[:, rows, :] = pieces[g, half:]
-
-    @pl.when(far_start() == 0)
-    def _():
-        outgoing[...] = high[...]
-
-    @pl.when(far_start() != 0)
-    def _():
-        outgoing[...] = low[...]
-
-
-def own_halves(pieces):
-    half = jax.ShapeDtypeStruct((PER // 2, WIDTH, LANES), jnp.bfloat16)
-    return pl.pallas_call(
-        own_kernel,
-        out_shape=(half,) * 3,
-        in_specs=[whole_vmem()],
-        out_specs=(whole_vmem(),) * 3,
-        compiler_params=pltpu.CompilerParams(vmem_limit_bytes=16 * MIB),
-        name="own_halves",
-    )(pieces)
+        for i in range(CHUNKS):
+            for k in range(2):
+                chunks[i][k, rows, :] = pieces[g, CHUNKS * k + i]
+    theirs = 1 - far_half(blk_place()[0])
+    for i in range(CHUNKS):
+        outgoing[i] = chunks[i][theirs]
+
+
+def own_chunks(pieces):
+    shapes = (blocks(2),) * CHUNKS + (blocks(CHUNKS),)
+    return small_kernel(own_kernel, "own_chunks", shapes, pieces)
+
+
+def pass_next(nexts, chosen):
+    def kernel(*refs):
+        theirs = 1 - far_half((blk_place()[0] + 3) % 4)
+        for j in range(len(chosen)):
+            refs[-1][j] = refs[j][theirs]
+
+    return small_kernel(kernel, "pass_next", blocks(len(chosen)), *[nexts[i] for i in chosen])
+
+
+def across_kernel(second, own, out):
+    out[...] = jnp.where(blk_place()[1] == 0, second[...], own[...])
+
+
+def for_across(second, own):
+    return small_kernel(across_kernel, "for_across", blocks(2), second, own)
+
+
+def pass_half_kernel(arrived, *refs):
+    seconds, out = refs[:-1], refs[-1]
+    x, l = blk_place()
+    for i in range(CHUNKS):
+        out[i] = jnp.where(l == 0, arrived[i], seconds[i][far_half(x)])
+
+
+def pass_half(arrived, seconds):
+    return small_kernel(pass_half_kernel, "pass_half", blocks(CHUNKS), arrived, *seconds)
 
 
 def correlate_one(mine, other):
@@ -199,76 +238,54 @@
     return (real * (1.0 / SPEC)).astype(jnp.bfloat16), (imag * (1.0 / SPEC)).astype(jnp.bfloat16)
 
 
-def correlate(own, items, before, half_count, arrived=None):
-    others = [other for _, _, other in items if other is not None]
-    has_far = arrived is not None
-    half, width, lanes = own[0].shape
+def correlate(name, own, arrays, jobs, before, half_count, with_far=False):
+    width, lanes = own[0].shape[1:]
+    count = len(list(jobs(arrays, True)))
 
     def kernel(*refs):
         refs = list(refs)
-        mine = (refs.pop(0), refs.pop(0))
-        sources = [mine[part] if other is None else refs.pop(0) for _, part, other in items]
-        arrived = refs.pop(0) if has_far else None
+        mine = [refs.pop(0) for _ in own]
+        sources = [refs.pop(0) for _ in arrays]
         if before is not None:
             refs.pop(0)
         out = refs.pop(0)
-        out_far = refs.pop(0) if has_far else None
-        results, sems = refs[:2]
+        out_far = refs.pop(0) if with_far else None
+        results, sems = refs
         copies = []
-        for j, (offset, part, _) in enumerate(items):
-            for c in range(half):
-                real, imag = correlate_one(mine[part][c], sources[j][c])
-                results[j, c, 0] = real
-                results[j, c, 1] = imag
-                copy = pltpu.make_async_copy(
-                    results.at[j, c], out.at[offset, part * half + c], sems.at[j, c]
-                )
-                copy.start()
-                copies.append(copy)
-        if has_far:
-            far_results, far_sems = refs[2:]
-            low = far_start() == 0
-            for c in range(half):
-                real, imag = correlate_one(jnp.where(low, mine[0][c], mine[1][c]), arrived[c])
-                far_results[c, 0] = real
-                far_results[c, 1] = imag
-                copy = pltpu.make_async_copy(far_results.at[c], out_far.at[c], far_sems.at[c])
-                copy.start()
-                copies.append(copy)
+        for j, (i, k, other, offset) in enumerate(jobs(sources, False)):
+            real, imag = correlate_one(mine[i][k], other)
+            results[j, 0] = real
+            results[j, 1] = imag
+            target = out_far.at[i] if offset is None else out.at[offset, CHUNKS * k + i]
+            copy = pltpu.make_async_copy(results.at[j], target, sems.at[j])
+            copy.start()
+            copies.append(copy)
         for copy in copies:
             copy.wait()
 
     near_shape = jax.ShapeDtypeStruct((half_count, PER, 2, width, width), jnp.bfloat16)
-    far_shape = jax.ShapeDtypeStruct((half, 2, width, width), jnp.bfloat16)
-    operands = [*own, *others] + ([arrived] if has_far else [])
+    far_shape = jax.ShapeDtypeStruct((CHUNKS, 2, width, width), jnp.bfloat16)
+    operands = [*own, *arrays]
     specs = [whole_vmem()] * len(operands)
     aliases = {}
     if before is not None:
         aliases = {len(operands): 0}
         operands.append(before)
         specs.append(pl.BlockSpec(memory_space=pl.ANY))
-    count = len(items)
-    scratch = [
-        VMEM((count, half, 2, width, width), jnp.bfloat16),
-        pltpu.SemaphoreType.DMA((count, half)),
-    ]
-    if has_far:
-        scratch += [VMEM((half, 2, width, width), jnp.bfloat16), pltpu.SemaphoreType.DMA((half,))]
-    channels = (count + has_far) * half
     return pl.pallas_call(
         kernel,
-        out_shape=(near_shape, far_shape) if has_far else near_shape,
+        out_shape=(near_shape, far_shape) if with_far else near_shape,
         in_specs=specs,
-        out_specs=(pl.BlockSpec(memory_space=pl.ANY),) * 2 if has_far else pl.BlockSpec(memory_space=pl.ANY),
+        out_specs=(pl.BlockSpec(memory_space=pl.ANY),) * 2 if with_far else pl.BlockSpec(memory_space=pl.ANY),
         input_output_aliases=aliases,
-        scratch_shapes=scratch,
+        scratch_shapes=[VMEM((count, 2, width, width), jnp.bfloat16), pltpu.SemaphoreType.DMA((count,))],
         cost_estimate=pl.CostEstimate(
-            flops=channels * 4 * width * width * lanes,
-            bytes_accessed=channels * 4 * width * width,
+            flops=count * 4 * width * width * lanes,
+            bytes_accessed=count * 4 * width * width,
             transcendentals=0,
         ),
         compiler_params=pltpu.CompilerParams(vmem_limit_bytes=24 * MIB),
-        name="correlate_" + "_".join(str(offset) for offset, _, _ in items),
+        name=name,
     )(*operands)
 
 
@@ -279,7 +296,6 @@
 LEFT = blk_route(lambda x, l: 2 * ((x - 1) % 4) + l)
 RIGHT = blk_route(lambda x, l: 2 * ((x + 1) % 4) + l)
 SWAP = blk_route(lambda x, l: 2 * x + 1 - l)
-BACK = blk_route(lambda x, l: (2 * x + l - 1) % 8)
 LEFT_ODD = blk_route(lambda x, l: 2 * ((x - l) % 4) + l)
 
 
@@ -293,24 +309,61 @@
 
 def on_device(samples, input_gains):
     half_count = lax.axis_size("blk") // 2
+    last = CHUNKS - 1
     pieces = channelize(samples[0], input_gains[0])
     pieces = lax.all_to_all(pieces, "grp", split_axis=0, concat_axis=0, tiled=True)
-    *own, outgoing = own_halves(pieces)
-    across, second, first, third = [], [], [], []
-    for part in range(2):
-        second.append(send(own[part], "blk", LEFT))
-        across.append(send(own[part], "blk", SWAP))
+    *own, outgoing = own_chunks(pieces)
+    leaving = list(own)
+    across = send(own[last], "blk", SWAP)
     passing = send(outgoing, "blk", RIGHT)
-    for part in range(2):
-        across[part], second[part] = all_arrived(across[part], second[part])
-        first.append(send(across[part], "blk", LEFT_ODD))
-        third.append(send(second[part], "blk", BACK))
+    second, nexts = [], []
+    for i in range(CHUNKS):
+        second.append(send(leaving[i], "blk", LEFT))
+        if i == 0:
+            second[i], leaving[2], leaving[3] = all_arrived(second[i], leaving[2], leaving[3])
+        if i == 1:
+            second[i], passing = all_arrived(second[i], passing)
+        if i == 2:
+            second[i], *nexts = all_arrived(second[i], *nexts)
+        if i < last:
+            nexts.append(send(for_across(second[i], own[i]), "blk", SWAP))
+    nexts.append(send(across, "blk", LEFT_ODD))
     arrived = send(passing, "blk", RIGHT)
-    vis_near = correlate(own, [(0, 0, None), (0, 1, None)], None, half_count)
-    vis_near = correlate(own, [(2, 0, second[0]), (2, 1, second[1])], vis_near, half_count)
-    vis_near = correlate(own, [(1, 0, first[0]), (3, 0, third[0])], vis_near, half_count)
-    last = [(1, 1, first[1]), (3, 1, third[1])]
-    vis_near, vis_far = correlate(own, last, vis_near, half_count, arrived)
+    third_a = send(pass_next(nexts, (0, 1)), "blk", LEFT)
+    third_b = send(pass_next(nexts, (2, 3)), "blk", LEFT)
+    third_half = send(pass_half(arrived, second), "blk", SWAP)
+
+    def same(refs, counting):
+        for i in range(CHUNKS):
+            for k in range(2):
+                yield i, k, None if counting else refs[i][k], 0
+
+    def second_and_far(refs, counting):
+        for i in range(CHUNKS):
+            for k in range(2):
+                yield i, k, None if counting else refs[i][k], 2
+        half = None if counting else far_half(blk_place()[0])
+        for i in range(CHUNKS):
+            yield i, half, None if counting else refs[CHUNKS][i], None
+
+    def first(refs, counting):
+        for i in range(CHUNKS):
+            for k in range(2):
+                yield i, k, None if counting else refs[i][k], 1
+
+    def third(refs, counting):
+        half = None if counting else far_half(blk_place()[0])
+        for i in range(CHUNKS):
+            yield i, None if counting else 1 - half, None if counting else refs[i // 2][i % 2], 3
+        for i in range(CHUNKS):
+            yield i, half, None if counting else refs[2][i], 3
+
+    vis_near = correlate("correlate_same", own, own, same, None, half_count)
+    vis_near, vis_far = correlate(
+        "correlate_second", own, [*second, arrived], second_and_far, vis_near, half_count, True
+    )
+    vis_near = correlate("correlate_first", own, nexts, first, vis_near, half_count)
+    vis_near = correlate("correlate_third", own, [third_a, third_b, third_half], third, vis_near, half_count)
     return (vis_near, vis_far)
 
 

time: 101 us -> 96.9 us (0.959)
  the two profiles are of different devices: /device:TPU:30 before, /device:TPU:48 now
where the time goes in v3:
time: 96.9 us; the launch traced here: 95.8 us
  blocking collectives  39 us (40%)
  starting transfers between devices  23.4 us (24%)
  waiting for transfers between devices  17.3 us (18%)
  Pallas kernels  14.6 us (15%)
    all_to_all x1, blocking collectives, on_device(): lax.all_to_all(pieces, 'grp', split_axis=0, concat_axis=0, tiled=True)  39 us
    ppermute x14, starting transfers between devices, send(): return lax.ppermute(block, axis, route)  23.4 us
    ppermute x14, waiting for transfers between devices, send(): return lax.ppermute(block, axis, route)  17.3 us
    pallas_call x1, Pallas kernels, channelize(): pl.pallas_call(channelize_kernel, out_shape=jax.ShapeDtypeStruct((GROUPS,...  7.31 us
    pallas_call x4, Pallas kernels, correlate(): pl.pallas_call(kernel, out_shape=(near_shape, far_shape) if with_far else...  6.95 us
  transfers between devices with their start and end apart: 14, of which 7 were waited for; matrix products, arithmetic and copies ran while one was open for 0% of the time, Pallas kernels for 6%

profile of v3, /device:TPU:48, one launch (start us, length us, event | category | flops | bytes accessed | tf_op | source)
XLA Modules:
  0.0 95.8 jit_solution(15703767837717197396)
XLA Ops:
  0.6 0.7 copy-done
  1.3 7.3 %channelize.1 = bf16[32,8,8,256]{3,2,1,0:T(8,128)(2,1)S(1)} custom-call(bf16[131,8,2048]{2,1,0:T(8,128)(2,1)} %bitcast.5, bf16[33,16,2048]{2,1,0:T(8,128)(2,1)} %constant.2.clone.table, f32[8,256]{1,0:T(8,128)S(1)} %bitcast.4), custom_call_target="tpu_custom_call" | custom-call | tf_op jit(solution)/shard_map/channelize/pallas_call | solution.py:147
  8.6 39.0 %all_to_all.5.pieces = bf16[32,8,8,256]{3,2,1,0:T(8,128)(2,1)S(1)} all-to-all(bf16[32,8,8,256]{3,2,1,0:T(8,128)(2,1)S(1)} %channelize.1), channel_id=1, replica_groups=mesh['grp'=32,'blk'=8] {'grp'}, dimensions={0} | all-to-all | bytes 2097152 | tf_op jit(solution)/shard_map/all_to_all | solution.py:314
  47.7 1.6 %collective-permute-start.4 = (bf16[4,256,256]{2,1,0:T(8,128)(2,1)S(1)}, bf16[4,256,256]{2,1,0:T(8,128)(2,1)S(1)}, u32[]{:S(2)}, u32[]{:S(2)}) collective-permute-start(bf16[4,256,256]{2,1,0:T(8,128)(2,1)S(1)} %get-tuple-element.23), channel_id=1, source_target_pairs={{0,2},{1,3},{2,4},{3,5},{4,6},{5,7},{6,0},{7,1},{8,10},{9,11},{10,... | collective-permute-start | bytes 1572872 | tf_op jit(solution)/shard_map/ppermute | solution.py:303
  49.3 1.7 %collective-permute-start.3 = (bf16[2,256,256]{2,1,0:T(8,128)(2,1)S(1)}, bf16[2,256,256]{2,1,0:T(8,128)(2,1)S(1)}, u32[]{:S(2)}, u32[]{:S(2)}) collective-permute-start(bf16[2,256,256]{2,1,0:T(8,128)(2,1)S(1)} %get-tuple-element.18.own.refs_1_.refs_5_), channel_id=1, source_target_pairs={{0,6},{1,7},{2,0},{3,1},{4,2},{5,3},{6,4},{7,5},{8,14},{9,15},{10,... | collective-permute-start | bytes 786440 | tf_op jit(solution)/shard_map/ppermute | solution.py:303
  51.1 1.6 %collective-permute-start = (bf16[2,256,256]{2,1,0:T(8,128)(2,1)S(1)}, bf16[2,256,256]{2,1,0:T(8,128)(2,1)S(1)}, u32[]{:S(2)}, u32[]{:S(2)}) collective-permute-start(bf16[2,256,256]{2,1,0:T(8,128)(2,1)S(1)} %get-tuple-element.17.own.refs_0_.refs_4_), channel_id=1, source_target_pairs={{0,6},{1,7},{2,0},{3,1},{4,2},{5,3},{6,4},{7,5},{8,14},{9,15},{10,... | collective-permute-start | bytes 786440 | tf_op jit(solution)/shard_map/ppermute | solution.py:303
  52.6 1.3 %collective-permute-start.8 = (bf16[2,256,256]{2,1,0:T(8,128)(2,1)S(1)}, bf16[2,256,256]{2,1,0:T(8,128)(2,1)S(1)}, u32[]{:S(2)}, u32[]{:S(2)}) collective-permute-start(bf16[2,256,256]{2,1,0:T(8,128)(2,1)S(1)} %get-tuple-element.29.refs_3_.refs_7_), channel_id=1, source_target_pairs={{0,1},{1,0},{2,3},{3,2},{4,5},{5,4},{6,7},{7,6},{8,9},{9,8},{10,11... | collective-permute-start | bytes 786440 | tf_op jit(solution)/shard_map/ppermute | solution.py:303
  53.9 4.6 %collective-permute-done.3.second.refs_1_.refs_5_ = bf16[2,256,256]{2,1,0:T(8,128)(2,1)S(1)} collective-permute-done((bf16[2,256,256]{2,1,0:T(8,128)(2,1)S(1)}, bf16[2,256,256]{2,1,0:T(8,128)(2,1)S(1)}, u32[]{:S(2)}, u32[]{:S(2)}) %collective-permute-start.3) | collective-permute-done | bytes 262176 | tf_op jit(solution)/shard_map/ppermute | solution.py:303
  58.5 4.3 %collective-permute-done.4 = bf16[4,256,256]{2,1,0:T(8,128)(2,1)S(1)} collective-permute-done((bf16[4,256,256]{2,1,0:T(8,128)(2,1)S(1)}, bf16[4,256,256]{2,1,0:T(8,128)(2,1)S(1)}, u32[]{:S(2)}, u32[]{:S(2)}) %collective-permute-start.4) | collective-permute-done | bytes 524320 | tf_op jit(solution)/shard_map/ppermute | solution.py:303
  63.2 1.4 %collective-permute-start.2 = (bf16[2,256,256]{2,1,0:T(8,128)(2,1)S(1)}, bf16[2,256,256]{2,1,0:T(8,128)(2,1)S(1)}, u32[]{:S(2)}, u32[]{:S(2)}) collective-permute-start(bf16[2,256,256]{2,1,0:T(8,128)(2,1)S(1)} %for_across.3), channel_id=1, source_target_pairs={{0,1},{1,0},{2,3},{3,2},{4,5},{5,4},{6,7},{7,6},{8,9},{9,8},{10,11... | collective-permute-start | bytes 786440 | tf_op jit(solution)/shard_map/ppermute | solution.py:303
  64.5 3.0 %collective-permute-start.1 = (bf16[2,256,256]{2,1,0:T(8,128)(2,1)S(1)}, bf16[2,256,256]{2,1,0:T(8,128)(2,1)S(1)}, u32[]{:S(2)}, u32[]{:S(2)}) collective-permute-start(bf16[2,256,256]{2,1,0:T(8,128)(2,1)S(1)} %get-tuple-element.21.own.refs_2_.refs_6_), channel_id=1, source_target_pairs={{0,6},{1,7},{2,0},{3,1},{4,2},{5,3},{6,4},{7,5},{8,14},{9,15},{10,... | collective-permute-start | bytes 786440 | tf_op jit(solution)/shard_map/ppermute | solution.py:303
  67.5 0.8 collective-permute-start.5
  68.7 3.3 %collective-permute-done.2.refs_0_.refs_4_ = bf16[2,256,256]{2,1,0:T(8,128)(2,1)S(1)} collective-permute-done((bf16[2,256,256]{2,1,0:T(8,128)(2,1)S(1)}, bf16[2,256,256]{2,1,0:T(8,128)(2,1)S(1)}, u32[]{:S(2)}, u32[]{:S(2)}) %collective-permute-start.2) | collective-permute-done | bytes 262176 | tf_op jit(solution)/shard_map/ppermute | solution.py:303
  72.7 1.5 %collective-permute-done.1.second.refs_2_.refs_6_ = bf16[2,256,256]{2,1,0:T(8,128)(2,1)S(1)} collective-permute-done((bf16[2,256,256]{2,1,0:T(8,128)(2,1)S(1)}, bf16[2,256,256]{2,1,0:T(8,128)(2,1)S(1)}, u32[]{:S(2)}, u32[]{:S(2)}) %collective-permute-start.1) | collective-permute-done | bytes 262176 | tf_op jit(solution)/shard_map/ppermute | solution.py:303
  74.2 1.7 %collective-permute-done.5.refs_1_.refs_5_ = bf16[2,256,256]{2,1,0:T(8,128)(2,1)S(1)} collective-permute-done((bf16[2,256,256]{2,1,0:T(8,128)(2,1)S(1)}, bf16[2,256,256]{2,1,0:T(8,128)(2,1)S(1)}, u32[]{:S(2)}, u32[]{:S(2)}) %collective-permute-start.5) | collective-permute-done | bytes 262176 | tf_op jit(solution)/shard_map/ppermute | solution.py:303
  75.9 3.0 %collective-permute-start.7 = (bf16[2,256,256]{2,1,0:T(8,128)(2,1)S(1)}, bf16[2,256,256]{2,1,0:T(8,128)(2,1)S(1)}, u32[]{:S(2)}, u32[]{:S(2)}) collective-permute-start(bf16[2,256,256]{2,1,0:T(8,128)(2,1)S(1)} %for_across.5), channel_id=1, source_target_pairs={{0,1},{1,0},{2,3},{3,2},{4,5},{5,4},{6,7},{7,6},{8,9},{9,8},{10,11... | collective-permute-start | bytes 786440 | tf_op jit(solution)/shard_map/ppermute | solution.py:303
  79.0 1.7 %collective-permute-start.13 = (bf16[4,256,256]{2,1,0:T(8,128)(2,1)S(1)}, bf16[4,256,256]{2,1,0:T(8,128)(2,1)S(1)}, u32[]{:S(2)}, u32[]{:S(2)}) collective-permute-start(bf16[4,256,256]{2,1,0:T(8,128)(2,1)S(1)} %pass_half.1), channel_id=1, source_target_pairs={{0,1},{1,0},{2,3},{3,2},{4,5},{5,4},{6,7},{7,6},{8,9},{9,8},{10,11... | collective-permute-start | bytes 1572872 | tf_op jit(solution)/shard_map/ppermute | solution.py:303
  80.8 3.8 %collective-permute-start.6 = (bf16[2,256,256]{2,1,0:T(8,128)(2,1)S(1)}, bf16[2,256,256]{2,1,0:T(8,128)(2,1)S(1)}, u32[]{:S(2)}, u32[]{:S(2)}) collective-permute-start(bf16[2,256,256]{2,1,0:T(8,128)(2,1)S(1)} %pass_next.2), channel_id=1, source_target_pairs={{0,6},{1,7},{2,0},{3,1},{4,2},{5,3},{6,4},{7,5},{8,14},{9,15},{10,... | collective-permute-start | bytes 786440 | tf_op jit(solution)/shard_map/ppermute | solution.py:303
  84.6 1.6 %collective-permute-done.7.refs_0_.refs_6_ = bf16[2,256,256]{2,1,0:T(8,128)(2,1)S(1)} collective-permute-done((bf16[2,256,256]{2,1,0:T(8,128)(2,1)S(1)}, bf16[2,256,256]{2,1,0:T(8,128)(2,1)S(1)}, u32[]{:S(2)}, u32[]{:S(2)}) %collective-permute-start.7) | collective-permute-done | bytes 262176 | tf_op jit(solution)/shard_map/ppermute | solution.py:303
  86.2 2.3 %collective-permute-start.10 = (bf16[2,256,256]{2,1,0:T(8,128)(2,1)S(1)}, bf16[2,256,256]{2,1,0:T(8,128)(2,1)S(1)}, u32[]{:S(2)}, u32[]{:S(2)}) collective-permute-start(bf16[2,256,256]{2,1,0:T(8,128)(2,1)S(1)} %pass_next.3), channel_id=1, source_target_pairs={{0,6},{1,7},{2,0},{3,1},{4,2},{5,3},{6,4},{7,5},{8,14},{9,15},{10,... | collective-permute-start | bytes 786440 | tf_op jit(solution)/shard_map/ppermute | solution.py:303
  88.5 1.6 %correlate_same.1.refs_9_ = bf16[4,8,2,256,256]{4,3,2,1,0:T(8,128)(2,1)} custom-call(bf16[2,256,256]{2,1,0:T(8,128)(2,1)S(1)} %get-tuple-element.17.own.refs_0_.refs_4_, bf16[2,256,256]{2,1,0:T(8,128)(2,1)S(1)} %get-tuple-element.18.own.refs_1_.refs_5_, bf16[2,256,256]{2,1,0:T(8,128)(2,1)S(1)} %get-tuple-element.21.own.refs_2_.refs_6_, ...), custom_call_target="tpu_custom_call" | custom-call | flops 536870912 | bytes 2097152 | tf_op jit(solution)/shard_map/correlate_same/pallas_call | solution.py:275
  90.2 2.0 %correlate_second.1 = (bf16[4,8,2,256,256]{4,3,2,1,0:T(8,128)(2,1)}, bf16[4,2,256,256]{3,2,1,0:T(8,128)(2,1)}) custom-call(bf16[2,256,256]{2,1,0:T(8,128)(2,1)S(1)} %get-tuple-element.17.own.refs_0_.refs_4_, bf16[2,256,256]{2,1,0:T(8,128)(2,1)S(1)} %get-tuple-element.18.own.refs_1_.refs_5_, ...), custom_call_target="tpu_custom_call", output_to_operand_aliasing={{0}: (9, {})} | custom-call | flops 805306368 | bytes 3145728 | tf_op jit(solution)/shard_map/correlate_second/pallas_call | solution.py:275
  92.2 1.6 %correlate_first.1.refs_7_ = bf16[4,8,2,256,256]{4,3,2,1,0:T(8,128)(2,1)} custom-call(bf16[2,256,256]{2,1,0:T(8,128)(2,1)S(1)} %get-tuple-element.17.own.refs_0_.refs_4_, bf16[2,256,256]{2,1,0:T(8,128)(2,1)S(1)} %get-tuple-element.18.own.refs_1_.refs_5_, ...), custom_call_target="tpu_custom_call", output_to_operand_aliasing={{}: (8, {})} | custom-call | flops 536870912 | bytes 2097152 | tf_op jit(solution)/shard_map/correlate_first/pallas_call | solution.py:275
  94.0 1.6 %correlate_third.1 = bf16[4,8,2,256,256]{4,3,2,1,0:T(8,128)(2,1)} custom-call(bf16[2,256,256]{2,1,0:T(8,128)(2,1)S(1)} %get-tuple-element.17.own.refs_0_.refs_4_, bf16[2,256,256]{2,1,0:T(8,128)(2,1)S(1)} %get-tuple-element.18.own.refs_1_.refs_5_, bf16[2,256,256]{2,1,0:T(8,128)(2,1)S(1)} %get-tuple-element.21.own.refs_2_.refs_6_, ...), custom_call_target="tpu_custom_call", output_to_operand_aliasing={{}: (7, {})} | custom-call | flops 536870912 | bytes 2097152 | tf_op jit(solution)/shard_map/correlate_third/pallas_call | solution.py:275
  (19 shorter events, 1.8 us)
Async XLA Ops:
  0.6 0.7 copy-start
  47.7 15.1 %collective-permute-start.4 = (bf16[4,256,256]{2,1,0:T(8,128)(2,1)S(1)}, bf16[4,256,256]{2,1,0:T(8,128)(2,1)S(1)}, u32[]{:S(2)}, u32[]{:S(2)}) collective-permute-start(bf16[4,256,256]{2,1,0:T(8,128)(2,1)S(1)} %get-tuple-element.23), channel_id=1, source_target_pairs={{0,2},{1,3},{2,4},{3,5},{4,6},{5,7},{6,0},{7,1},{8,10},{9,11},{10,... | collective-permute-start | bytes 1572872 | tf_op jit(solution)/shard_map/ppermute | solution.py:303
  49.3 9.2 %collective-permute-start.3 = (bf16[2,256,256]{2,1,0:T(8,128)(2,1)S(1)}, bf16[2,256,256]{2,1,0:T(8,128)(2,1)S(1)}, u32[]{:S(2)}, u32[]{:S(2)}) collective-permute-start(bf16[2,256,256]{2,1,0:T(8,128)(2,1)S(1)} %get-tuple-element.18.own.refs_1_.refs_5_), channel_id=1, source_target_pairs={{0,6},{1,7},{2,0},{3,1},{4,2},{5,3},{6,4},{7,5},{8,14},{9,15},{10,... | collective-permute-start | bytes 786440 | tf_op jit(solution)/shard_map/ppermute | solution.py:303
  51.1 12.1 %collective-permute-start = (bf16[2,256,256]{2,1,0:T(8,128)(2,1)S(1)}, bf16[2,256,256]{2,1,0:T(8,128)(2,1)S(1)}, u32[]{:S(2)}, u32[]{:S(2)}) collective-permute-start(bf16[2,256,256]{2,1,0:T(8,128)(2,1)S(1)} %get-tuple-element.17.own.refs_0_.refs_4_), channel_id=1, source_target_pairs={{0,6},{1,7},{2,0},{3,1},{4,2},{5,3},{6,4},{7,5},{8,14},{9,15},{10,... | collective-permute-start | bytes 786440 | tf_op jit(solution)/shard_map/ppermute | solution.py:303
  52.6 15.7 %collective-permute-start.8 = (bf16[2,256,256]{2,1,0:T(8,128)(2,1)S(1)}, bf16[2,256,256]{2,1,0:T(8,128)(2,1)S(1)}, u32[]{:S(2)}, u32[]{:S(2)}) collective-permute-start(bf16[2,256,256]{2,1,0:T(8,128)(2,1)S(1)} %get-tuple-element.29.refs_3_.refs_7_), channel_id=1, source_target_pairs={{0,1},{1,0},{2,3},{3,2},{4,5},{5,4},{6,7},{7,6},{8,9},{9,8},{10,11... | collective-permute-start | bytes 786440 | tf_op jit(solution)/shard_map/ppermute | solution.py:303
  62.8 16.1 %collective-permute-start.11 = (bf16[4,256,256]{2,1,0:T(8,128)(2,1)S(1)}, bf16[4,256,256]{2,1,0:T(8,128)(2,1)S(1)}, u32[]{:S(2)}, u32[]{:S(2)}) collective-permute-start(bf16[4,256,256]{2,1,0:T(8,128)(2,1)S(1)} %collective-permute-done.4), channel_id=1, source_target_pairs={{0,2},{1,3},{2,4},{3,5},{4,6},{5,7},{6,0},{7,1},{8,10},{9,11},{10,... | collective-permute-start | bytes 1572872 | tf_op jit(solution)/shard_map/ppermute | solution.py:303
  63.2 8.9 %collective-permute-start.2 = (bf16[2,256,256]{2,1,0:T(8,128)(2,1)S(1)}, bf16[2,256,256]{2,1,0:T(8,128)(2,1)S(1)}, u32[]{:S(2)}, u32[]{:S(2)}) collective-permute-start(bf16[2,256,256]{2,1,0:T(8,128)(2,1)S(1)} %for_across.3), channel_id=1, source_target_pairs={{0,1},{1,0},{2,3},{3,2},{4,5},{5,4},{6,7},{7,6},{8,9},{9,8},{10,11... | collective-permute-start | bytes 786440 | tf_op jit(solution)/shard_map/ppermute | solution.py:303
  64.5 9.7 %collective-permute-start.1 = (bf16[2,256,256]{2,1,0:T(8,128)(2,1)S(1)}, bf16[2,256,256]{2,1,0:T(8,128)(2,1)S(1)}, u32[]{:S(2)}, u32[]{:S(2)}) collective-permute-start(bf16[2,256,256]{2,1,0:T(8,128)(2,1)S(1)} %get-tuple-element.21.own.refs_2_.refs_6_), channel_id=1, source_target_pairs={{0,6},{1,7},{2,0},{3,1},{4,2},{5,3},{6,4},{7,5},{8,14},{9,15},{10,... | collective-permute-start | bytes 786440 | tf_op jit(solution)/shard_map/ppermute | solution.py:303
  67.5 8.4 %collective-permute-start.5 = (bf16[2,256,256]{2,1,0:T(8,128)(2,1)S(1)}, bf16[2,256,256]{2,1,0:T(8,128)(2,1)S(1)}, u32[]{:S(2)}, u32[]{:S(2)}) collective-permute-start(bf16[2,256,256]{2,1,0:T(8,128)(2,1)S(1)} %for_across.4), channel_id=1, source_target_pairs={{0,1},{1,0},{2,3},{3,2},{4,5},{5,4},{6,7},{7,6},{8,9},{9,8},{10,11... | collective-permute-start | bytes 786440 | tf_op jit(solution)/shard_map/ppermute | solution.py:303
  68.4 10.6 %collective-permute-start.12 = (bf16[2,256,256]{2,1,0:T(8,128)(2,1)S(1)}, bf16[2,256,256]{2,1,0:T(8,128)(2,1)S(1)}, u32[]{:S(2)}, u32[]{:S(2)}) collective-permute-start(bf16[2,256,256]{2,1,0:T(8,128)(2,1)S(1)} %get-tuple-element.29.refs_3_.refs_7_), channel_id=1, source_target_pairs={{0,6},{1,7},{2,0},{3,1},{4,2},{5,3},{6,4},{7,5},{8,14},{9,15},{10,... | collective-permute-start | bytes 786440 | tf_op jit(solution)/shard_map/ppermute | solution.py:303
  72.0 12.5 %collective-permute-start.9 = (bf16[2,256,256]{2,1,0:T(8,128)(2,1)S(1)}, bf16[2,256,256]{2,1,0:T(8,128)(2,1)S(1)}, u32[]{:S(2)}, u32[]{:S(2)}) collective-permute-start(bf16[2,256,256]{2,1,0:T(8,128)(2,1)S(1)} %collective-permute-done.8), channel_id=1, source_target_pairs={{0,0},{1,7},{2,2},{3,1},{4,4},{5,3},{6,6},{7,5},{8,8},{9,15},{10,1... | collective-permute-start | bytes 786440 | tf_op jit(solution)/shard_map/ppermute | solution.py:303
  75.9 10.2 %collective-permute-start.7 = (bf16[2,256,256]{2,1,0:T(8,128)(2,1)S(1)}, bf16[2,256,256]{2,1,0:T(8,128)(2,1)S(1)}, u32[]{:S(2)}, u32[]{:S(2)}) collective-permute-start(bf16[2,256,256]{2,1,0:T(8,128)(2,1)S(1)} %for_across.5), channel_id=1, source_target_pairs={{0,1},{1,0},{2,3},{3,2},{4,5},{5,4},{6,7},{7,6},{8,9},{9,8},{10,11... | collective-permute-start | bytes 786440 | tf_op jit(solution)/shard_map/ppermute | solution.py:303
  79.0 15.0 %collective-permute-start.13 = (bf16[4,256,256]{2,1,0:T(8,128)(2,1)S(1)}, bf16[4,256,256]{2,1,0:T(8,128)(2,1)S(1)}, u32[]{:S(2)}, u32[]{:S(2)}) collective-permute-start(bf16[4,256,256]{2,1,0:T(8,128)(2,1)S(1)} %pass_half.1), channel_id=1, source_target_pairs={{0,1},{1,0},{2,3},{3,2},{4,5},{5,4},{6,7},{7,6},{8,9},{9,8},{10,11... | collective-permute-start | bytes 1572872 | tf_op jit(solution)/shard_map/ppermute | solution.py:303
  80.8 13.1 %collective-permute-start.6 = (bf16[2,256,256]{2,1,0:T(8,128)(2,1)S(1)}, bf16[2,256,256]{2,1,0:T(8,128)(2,1)S(1)}, u32[]{:S(2)}, u32[]{:S(2)}) collective-permute-start(bf16[2,256,256]{2,1,0:T(8,128)(2,1)S(1)} %pass_next.2), channel_id=1, source_target_pairs={{0,6},{1,7},{2,0},{3,1},{4,2},{5,3},{6,4},{7,5},{8,14},{9,15},{10,... | collective-permute-start | bytes 786440 | tf_op jit(solution)/shard_map/ppermute | solution.py:303
  86.2 7.7 %collective-permute-start.10 = (bf16[2,256,256]{2,1,0:T(8,128)(2,1)S(1)}, bf16[2,256,256]{2,1,0:T(8,128)(2,1)S(1)}, u32[]{:S(2)}, u32[]{:S(2)}) collective-permute-start(bf16[2,256,256]{2,1,0:T(8,128)(2,1)S(1)} %pass_next.3), channel_id=1, source_target_pairs={{0,6},{1,7},{2,0},{3,1},{4,2},{5,3},{6,4},{7,5},{8,14},{9,15},{10,... | collective-permute-start | bytes 786440 | tf_op jit(solution)/shard_map/ppermute | solution.py:303

commit v4 on v3

--- a/solution.py
+++ b/solution.py
@@ -186,7 +186,7 @@
 
 
 def own_kernel(pieces, *outs):
-    chunks, outgoing = outs[:CHUNKS], outs[CHUNKS]
+    chunks, outgoing = outs[:CHUNKS], outs[CHUNKS:]
     for g in range(GROUPS):
         rows = slice(g * SHARE, (g + 1) * SHARE)
         for i in range(CHUNKS):
@@ -194,11 +194,11 @@
                 chunks[i][k, rows, :] = pieces[g, CHUNKS * k + i]
     theirs = 1 - far_half(blk_place()[0])
     for i in range(CHUNKS):
-        outgoing[i] = chunks[i][theirs]
+        outgoing[i // 2][i % 2] = chunks[i][theirs]
 
 
 def own_chunks(pieces):
-    shapes = (blocks(2),) * CHUNKS + (blocks(CHUNKS),)
+    shapes = (blocks(2),) * (CHUNKS + 2)
     return small_kernel(own_kernel, "own_chunks", shapes, pieces)
 
 
@@ -219,15 +219,15 @@
     return small_kernel(across_kernel, "for_across", blocks(2), second, own)
 
 
-def pass_half_kernel(arrived, *refs):
-    seconds, out = refs[:-1], refs[-1]
+def pass_half_kernel(*refs):
+    arrived, seconds, out = refs[:2], refs[2:-1], refs[-1]
     x, l = blk_place()
     for i in range(CHUNKS):
-        out[i] = jnp.where(l == 0, arrived[i], seconds[i][far_half(x)])
+        out[i] = jnp.where(l == 0, arrived[i // 2][i % 2], seconds[i][far_half(x)])
 
 
 def pass_half(arrived, seconds):
-    return small_kernel(pass_half_kernel, "pass_half", blocks(CHUNKS), arrived, *seconds)
+    return small_kernel(pass_half_kernel, "pass_half", blocks(CHUNKS), *arrived, *seconds)
 
 
 def correlate_one(mine, other):
@@ -312,23 +312,26 @@
     last = CHUNKS - 1
     pieces = channelize(samples[0], input_gains[0])
     pieces = lax.all_to_all(pieces, "grp", split_axis=0, concat_axis=0, tiled=True)
-    *own, outgoing = own_chunks(pieces)
+    *own, out_a, out_b = own_chunks(pieces)
     leaving = list(own)
     across = send(own[last], "blk", SWAP)
-    passing = send(outgoing, "blk", RIGHT)
+    pass_a = send(out_a, "blk", RIGHT)
+    pass_b = send(out_b, "blk", RIGHT)
     second, nexts = [], []
     for i in range(CHUNKS):
         second.append(send(leaving[i], "blk", LEFT))
         if i == 0:
             second[i], leaving[2], leaving[3] = all_arrived(second[i], leaving[2], leaving[3])
         if i == 1:
-            second[i], passing = all_arrived(second[i], passing)
+            second[i], pass_a = all_arrived(second[i], pass_a)
         if i == 2:
             second[i], *nexts = all_arrived(second[i], *nexts)
+        if i == 1:
+            _, _, pass_b = all_arrived(second[0], second[1], pass_b)
         if i < last:
             nexts.append(send(for_across(second[i], own[i]), "blk", SWAP))
     nexts.append(send(across, "blk", LEFT_ODD))
-    arrived = send(passing, "blk", RIGHT)
+    arrived = [send(pass_a, "blk", RIGHT), send(pass_b, "blk", RIGHT)]
     third_a = send(pass_next(nexts, (0, 1)), "blk", LEFT)
     third_b = send(pass_next(nexts, (2, 3)), "blk", LEFT)
     third_half = send(pass_half(arrived, second), "blk", SWAP)
@@ -344,7 +347,7 @@
                 yield i, k, None if counting else refs[i][k], 2
         half = None if counting else far_half(blk_place()[0])
         for i in range(CHUNKS):
-            yield i, half, None if counting else refs[CHUNKS][i], None
+            yield i, half, None if counting else refs[CHUNKS + i // 2][i % 2], None
 
     def first(refs, counting):
         for i in range(CHUNKS):
@@ -360,7 +363,7 @@
 
     vis_near = correlate("correlate_same", own, own, same, None, half_count)
     vis_near, vis_far = correlate(
-        "correlate_second", own, [*second, arrived], second_and_far, vis_near, half_count, True
+        "correlate_second", own, [*second, *arrived], second_and_far, vis_near, half_count, True
     )
     vis_near = correlate("correlate_first", own, nexts, first, vis_near, half_count)
     vis_near = correlate("correlate_third", own, [third_a, third_b, third_half], third, vis_near, half_count)

time: 96.9 us -> 97 us (level)
  starting transfers between devices: 23.4 us -> 25.4 us
  waiting for transfers between devices: 17.3 us -> 16.2 us
    ppermute x14 -> x16, starting transfers between devices: 23.4 us -> 25.4 us  [send(): return lax.ppermute(block, axis, route)]
    ppermute x14 -> x16, waiting for transfers between devices: 17.3 us -> 16.2 us  [send(): return lax.ppermute(block, axis, route)]
  transfers between devices with their start and end apart: 14 -> 16, of which waited for: 7 -> 7; matrix products, arithmetic and copies ran while one was open for 0% -> 0% of each run, Pallas kernels for 6% -> 6%
where the time goes in v4:
time: 97 us; the launch traced here: 96.8 us
  blocking collectives  39 us (40%)
  starting transfers between devices  25.4 us (26%)
  waiting for transfers between devices  16.2 us (17%)
  Pallas kernels  14.6 us (15%)
    all_to_all x1, blocking collectives, on_device(): lax.all_to_all(pieces, 'grp', split_axis=0, concat_axis=0, tiled=True)  39 us
    ppermute x16, starting transfers between devices, send(): return lax.ppermute(block, axis, route)  25.4 us
    ppermute x16, waiting for transfers between devices, send(): return lax.ppermute(block, axis, route)  16.2 us
    pallas_call x1, Pallas kernels, channelize(): pl.pallas_call(channelize_kernel, out_shape=jax.ShapeDtypeStruct((GROUPS,...  7.31 us
    pallas_call x4, Pallas kernels, correlate(): pl.pallas_call(kernel, out_shape=(near_shape, far_shape) if with_far else...  6.96 us
  transfers between devices with their start and end apart: 16, of which 7 were waited for; matrix products, arithmetic and copies ran while one was open for 0% of the time, Pallas kernels for 6%

profile of v4, /device:TPU:48, one launch (start us, length us, event | category | flops | bytes accessed | tf_op | source)
XLA Modules:
  0.0 96.8 jit_solution(2900864637826443755)
XLA Ops:
  1.3 7.3 %channelize.1 = bf16[32,8,8,256]{3,2,1,0:T(8,128)(2,1)S(1)} custom-call(bf16[131,8,2048]{2,1,0:T(8,128)(2,1)} %bitcast.5, bf16[33,16,2048]{2,1,0:T(8,128)(2,1)} %constant.2.clone.table, f32[8,256]{1,0:T(8,128)S(1)} %bitcast.4), custom_call_target="tpu_custom_call" | custom-call | tf_op jit(solution)/shard_map/channelize/pallas_call | solution.py:147
  8.6 39.0 %all_to_all.5.pieces = bf16[32,8,8,256]{3,2,1,0:T(8,128)(2,1)S(1)} all-to-all(bf16[32,8,8,256]{3,2,1,0:T(8,128)(2,1)S(1)} %channelize.1), channel_id=1, replica_groups=mesh['grp'=32,'blk'=8] {'grp'}, dimensions={0} | all-to-all | bytes 2097152 | tf_op jit(solution)/shard_map/all_to_all | solution.py:314
  47.7 2.8 %collective-permute-start = (bf16[2,256,256]{2,1,0:T(8,128)(2,1)S(1)}, bf16[2,256,256]{2,1,0:T(8,128)(2,1)S(1)}, u32[]{:S(2)}, u32[]{:S(2)}) collective-permute-start(bf16[2,256,256]{2,1,0:T(8,128)(2,1)S(1)} %get-tuple-element.19.own.refs_0_.refs_4_), channel_id=1, source_target_pairs={{0,6},{1,7},{2,0},{3,1},{4,2},{5,3},{6,4},{7,5},{8,14},{9,15},{10,... | collective-permute-start | bytes 786440 | tf_op jit(solution)/shard_map/ppermute | solution.py:303
  50.6 0.8 collective-permute-start.3
  51.4 1.2 %collective-permute-start.4 = (bf16[2,256,256]{2,1,0:T(8,128)(2,1)S(1)}, bf16[2,256,256]{2,1,0:T(8,128)(2,1)S(1)}, u32[]{:S(2)}, u32[]{:S(2)}) collective-permute-start(bf16[2,256,256]{2,1,0:T(8,128)(2,1)S(1)} %get-tuple-element.25), channel_id=1, source_target_pairs={{0,2},{1,3},{2,4},{3,5},{4,6},{5,7},{6,0},{7,1},{8,10},{9,11},{10,... | collective-permute-start | bytes 786440 | tf_op jit(solution)/shard_map/ppermute | solution.py:303
  52.6 1.3 %collective-permute-start.8 = (bf16[2,256,256]{2,1,0:T(8,128)(2,1)S(1)}, bf16[2,256,256]{2,1,0:T(8,128)(2,1)S(1)}, u32[]{:S(2)}, u32[]{:S(2)}) collective-permute-start(bf16[2,256,256]{2,1,0:T(8,128)(2,1)S(1)} %get-tuple-element.33.refs_3_.refs_7_), channel_id=1, source_target_pairs={{0,1},{1,0},{2,3},{3,2},{4,5},{5,4},{6,7},{7,6},{8,9},{9,8},{10,11... | collective-permute-start | bytes 786440 | tf_op jit(solution)/shard_map/ppermute | solution.py:303
  53.9 3.4 %collective-permute-done.second.refs_2_.refs_4_ = bf16[2,256,256]{2,1,0:T(8,128)(2,1)S(1)} collective-permute-done((bf16[2,256,256]{2,1,0:T(8,128)(2,1)S(1)}, bf16[2,256,256]{2,1,0:T(8,128)(2,1)S(1)}, u32[]{:S(2)}, u32[]{:S(2)}) %collective-permute-start) | collective-permute-done | bytes 262176 | tf_op jit(solution)/shard_map/ppermute | solution.py:303
  57.3 1.4 %collective-permute-start.2 = (bf16[2,256,256]{2,1,0:T(8,128)(2,1)S(1)}, bf16[2,256,256]{2,1,0:T(8,128)(2,1)S(1)}, u32[]{:S(2)}, u32[]{:S(2)}) collective-permute-start(bf16[2,256,256]{2,1,0:T(8,128)(2,1)S(1)} %for_across.3), channel_id=1, source_target_pairs={{0,1},{1,0},{2,3},{3,2},{4,5},{5,4},{6,7},{7,6},{8,9},{9,8},{10,11... | collective-permute-start | bytes 786440 | tf_op jit(solution)/shard_map/ppermute | solution.py:303
  58.7 3.2 %collective-permute-done.3.second.refs_3_.refs_5_ = bf16[2,256,256]{2,1,0:T(8,128)(2,1)S(1)} collective-permute-done((bf16[2,256,256]{2,1,0:T(8,128)(2,1)S(1)}, bf16[2,256,256]{2,1,0:T(8,128)(2,1)S(1)}, u32[]{:S(2)}, u32[]{:S(2)}) %collective-permute-start.3) | collective-permute-done | bytes 262176 | tf_op jit(solution)/shard_map/ppermute | solution.py:303
  61.9 3.7 %collective-permute-start.1 = (bf16[2,256,256]{2,1,0:T(8,128)(2,1)S(1)}, bf16[2,256,256]{2,1,0:T(8,128)(2,1)S(1)}, u32[]{:S(2)}, u32[]{:S(2)}) collective-permute-start(bf16[2,256,256]{2,1,0:T(8,128)(2,1)S(1)} %get-tuple-element.23.own.refs_2_.refs_6_), channel_id=1, source_target_pairs={{0,6},{1,7},{2,0},{3,1},{4,2},{5,3},{6,4},{7,5},{8,14},{9,15},{10,... | collective-permute-start | bytes 786440 | tf_op jit(solution)/shard_map/ppermute | solution.py:303
  65.6 1.4 %collective-permute-start.5 = (bf16[2,256,256]{2,1,0:T(8,128)(2,1)S(1)}, bf16[2,256,256]{2,1,0:T(8,128)(2,1)S(1)}, u32[]{:S(2)}, u32[]{:S(2)}) collective-permute-start(bf16[2,256,256]{2,1,0:T(8,128)(2,1)S(1)} %for_across.4), channel_id=1, source_target_pairs={{0,1},{1,0},{2,3},{3,2},{4,5},{5,4},{6,7},{7,6},{8,9},{9,8},{10,11... | collective-permute-start | bytes 786440 | tf_op jit(solution)/shard_map/ppermute | solution.py:303
  67.0 3.2 %collective-permute-start.14 = (bf16[2,256,256]{2,1,0:T(8,128)(2,1)S(1)}, bf16[2,256,256]{2,1,0:T(8,128)(2,1)S(1)}, u32[]{:S(2)}, u32[]{:S(2)}) collective-permute-start(bf16[2,256,256]{2,1,0:T(8,128)(2,1)S(1)} %get-tuple-element.33.refs_3_.refs_7_), channel_id=1, source_target_pairs={{0,6},{1,7},{2,0},{3,1},{4,2},{5,3},{6,4},{7,5},{8,14},{9,15},{10,... | collective-permute-start | bytes 786440 | tf_op jit(solution)/shard_map/ppermute | solution.py:303
  70.3 1.9 %collective-permute-done.1.second.refs_4_.refs_6_ = bf16[2,256,256]{2,1,0:T(8,128)(2,1)S(1)} collective-permute-done((bf16[2,256,256]{2,1,0:T(8,128)(2,1)S(1)}, bf16[2,256,256]{2,1,0:T(8,128)(2,1)S(1)}, u32[]{:S(2)}, u32[]{:S(2)}) %collective-permute-start.1) | collective-permute-done | bytes 262176 | tf_op jit(solution)/shard_map/ppermute | solution.py:303
  72.9 6.5 %collective-permute-start.7 = (bf16[2,256,256]{2,1,0:T(8,128)(2,1)S(1)}, bf16[2,256,256]{2,1,0:T(8,128)(2,1)S(1)}, u32[]{:S(2)}, u32[]{:S(2)}) collective-permute-start(bf16[2,256,256]{2,1,0:T(8,128)(2,1)S(1)} %for_across.5), channel_id=1, source_target_pairs={{0,1},{1,0},{2,3},{3,2},{4,5},{5,4},{6,7},{7,6},{8,9},{9,8},{10,11... | collective-permute-start | bytes 786440 | tf_op jit(solution)/shard_map/ppermute | solution.py:303
  79.4 1.2 %collective-permute-done.11.refs_0_.refs_8_ = bf16[2,256,256]{2,1,0:T(8,128)(2,1)S(1)} collective-permute-done((bf16[2,256,256]{2,1,0:T(8,128)(2,1)S(1)}, bf16[2,256,256]{2,1,0:T(8,128)(2,1)S(1)}, u32[]{:S(2)}, u32[]{:S(2)}) %collective-permute-start.11) | collective-permute-done | bytes 262176 | tf_op jit(solution)/shard_map/ppermute | solution.py:303
  80.7 0.8 collective-permute-start.15
  81.5 1.5 %collective-permute-start.6 = (bf16[2,256,256]{2,1,0:T(8,128)(2,1)S(1)}, bf16[2,256,256]{2,1,0:T(8,128)(2,1)S(1)}, u32[]{:S(2)}, u32[]{:S(2)}) collective-permute-start(bf16[2,256,256]{2,1,0:T(8,128)(2,1)S(1)} %pass_next.2), channel_id=1, source_target_pairs={{0,6},{1,7},{2,0},{3,1},{4,2},{5,3},{6,4},{7,5},{8,14},{9,15},{10,... | collective-permute-start | bytes 786440 | tf_op jit(solution)/shard_map/ppermute | solution.py:303
  83.0 3.5 %collective-permute-done.7.refs_0_.refs_6_ = bf16[2,256,256]{2,1,0:T(8,128)(2,1)S(1)} collective-permute-done((bf16[2,256,256]{2,1,0:T(8,128)(2,1)S(1)}, bf16[2,256,256]{2,1,0:T(8,128)(2,1)S(1)}, u32[]{:S(2)}, u32[]{:S(2)}) %collective-permute-start.7) | collective-permute-done | bytes 262176 | tf_op jit(solution)/shard_map/ppermute | solution.py:303
  86.6 1.6 %correlate_same.1.refs_10_ = bf16[4,8,2,256,256]{4,3,2,1,0:T(8,128)(2,1)} custom-call(bf16[2,256,256]{2,1,0:T(8,128)(2,1)S(1)} %get-tuple-element.19.own.refs_0_.refs_4_, bf16[2,256,256]{2,1,0:T(8,128)(2,1)S(1)} %get-tuple-element.20.own.refs_1_.refs_5_, bf16[2,256,256]{2,1,0:T(8,128)(2,1)S(1)} %get-tuple-element.23.own.refs_2_.refs_6_, ...), custom_call_target="tpu_custom_call" | custom-call | flops 536870912 | bytes 2097152 | tf_op jit(solution)/shard_map/correlate_same/pallas_call | solution.py:275
  88.3 2.0 %correlate_second.1 = (bf16[4,8,2,256,256]{4,3,2,1,0:T(8,128)(2,1)}, bf16[4,2,256,256]{3,2,1,0:T(8,128)(2,1)}) custom-call(bf16[2,256,256]{2,1,0:T(8,128)(2,1)S(1)} %get-tuple-element.19.own.refs_0_.refs_4_, bf16[2,256,256]{2,1,0:T(8,128)(2,1)S(1)} %get-tuple-element.20.own.refs_1_.refs_5_, ...), custom_call_target="tpu_custom_call", output_to_operand_aliasing={{0}: (10, {})} | custom-call | flops 805306368 | bytes 3145728 | tf_op jit(solution)/shard_map/correlate_second/pallas_call | solution.py:275
  90.3 1.6 %correlate_first.1.refs_7_ = bf16[4,8,2,256,256]{4,3,2,1,0:T(8,128)(2,1)} custom-call(bf16[2,256,256]{2,1,0:T(8,128)(2,1)S(1)} %get-tuple-element.19.own.refs_0_.refs_4_, bf16[2,256,256]{2,1,0:T(8,128)(2,1)S(1)} %get-tuple-element.20.own.refs_1_.refs_5_, ...), custom_call_target="tpu_custom_call", output_to_operand_aliasing={{}: (8, {})} | custom-call | flops 536870912 | bytes 2097152 | tf_op jit(solution)/shard_map/correlate_first/pallas_call | solution.py:275
  92.0 1.0 collective-permute-done.10.refs_5_
  93.0 2.0 %collective-permute-done.15.refs_6_ = bf16[4,256,256]{2,1,0:T(8,128)(2,1)S(1)} collective-permute-done((bf16[4,256,256]{2,1,0:T(8,128)(2,1)S(1)}, bf16[4,256,256]{2,1,0:T(8,128)(2,1)S(1)}, u32[]{:S(2)}, u32[]{:S(2)}) %collective-permute-start.15) | collective-permute-done | bytes 524320 | tf_op jit(solution)/shard_map/ppermute | solution.py:303
  95.0 1.6 %correlate_third.1 = bf16[4,8,2,256,256]{4,3,2,1,0:T(8,128)(2,1)} custom-call(bf16[2,256,256]{2,1,0:T(8,128)(2,1)S(1)} %get-tuple-element.19.own.refs_0_.refs_4_, bf16[2,256,256]{2,1,0:T(8,128)(2,1)S(1)} %get-tuple-element.20.own.refs_1_.refs_5_, bf16[2,256,256]{2,1,0:T(8,128)(2,1)S(1)} %get-tuple-element.23.own.refs_2_.refs_6_, ...), custom_call_target="tpu_custom_call", output_to_operand_aliasing={{}: (7, {})} | custom-call | flops 536870912 | bytes 2097152 | tf_op jit(solution)/shard_map/correlate_third/pallas_call | solution.py:275
  (23 shorter events, 1.8 us)
Async XLA Ops:
  0.6 0.7 copy-start
  47.7 9.5 %collective-permute-start = (bf16[2,256,256]{2,1,0:T(8,128)(2,1)S(1)}, bf16[2,256,256]{2,1,0:T(8,128)(2,1)S(1)}, u32[]{:S(2)}, u32[]{:S(2)}) collective-permute-start(bf16[2,256,256]{2,1,0:T(8,128)(2,1)S(1)} %get-tuple-element.19.own.refs_0_.refs_4_), channel_id=1, source_target_pairs={{0,6},{1,7},{2,0},{3,1},{4,2},{5,3},{6,4},{7,5},{8,14},{9,15},{10,... | collective-permute-start | bytes 786440 | tf_op jit(solution)/shard_map/ppermute | solution.py:303
  50.6 11.3 %collective-permute-start.3 = (bf16[2,256,256]{2,1,0:T(8,128)(2,1)S(1)}, bf16[2,256,256]{2,1,0:T(8,128)(2,1)S(1)}, u32[]{:S(2)}, u32[]{:S(2)}) collective-permute-start(bf16[2,256,256]{2,1,0:T(8,128)(2,1)S(1)} %get-tuple-element.20.own.refs_1_.refs_5_), channel_id=1, source_target_pairs={{0,6},{1,7},{2,0},{3,1},{4,2},{5,3},{6,4},{7,5},{8,14},{9,15},{10,... | collective-permute-start | bytes 786440 | tf_op jit(solution)/shard_map/ppermute | solution.py:303
  51.4 14.2 %collective-permute-start.4 = (bf16[2,256,256]{2,1,0:T(8,128)(2,1)S(1)}, bf16[2,256,256]{2,1,0:T(8,128)(2,1)S(1)}, u32[]{:S(2)}, u32[]{:S(2)}) collective-permute-start(bf16[2,256,256]{2,1,0:T(8,128)(2,1)S(1)} %get-tuple-element.25), channel_id=1, source_target_pairs={{0,2},{1,3},{2,4},{3,5},{4,6},{5,7},{6,0},{7,1},{8,10},{9,11},{10,... | collective-permute-start | bytes 786440 | tf_op jit(solution)/shard_map/ppermute | solution.py:303
  52.6 14.4 %collective-permute-start.12 = (bf16[2,256,256]{2,1,0:T(8,128)(2,1)S(1)}, bf16[2,256,256]{2,1,0:T(8,128)(2,1)S(1)}, u32[]{:S(2)}, u32[]{:S(2)}) collective-permute-start(bf16[2,256,256]{2,1,0:T(8,128)(2,1)S(1)} %get-tuple-element.31), channel_id=1, source_target_pairs={{0,2},{1,3},{2,4},{3,5},{4,6},{5,7},{6,0},{7,1},{8,10},{9,11},{10,... | collective-permute-start | bytes 786440 | tf_op jit(solution)/shard_map/ppermute | solution.py:303
  52.6 14.4 %collective-permute-start.8 = (bf16[2,256,256]{2,1,0:T(8,128)(2,1)S(1)}, bf16[2,256,256]{2,1,0:T(8,128)(2,1)S(1)}, u32[]{:S(2)}, u32[]{:S(2)}) collective-permute-start(bf16[2,256,256]{2,1,0:T(8,128)(2,1)S(1)} %get-tuple-element.33.refs_3_.refs_7_), channel_id=1, source_target_pairs={{0,1},{1,0},{2,3},{3,2},{4,5},{5,4},{6,7},{7,6},{8,9},{9,8},{10,11... | collective-permute-start | bytes 786440 | tf_op jit(solution)/shard_map/ppermute | solution.py:303
  57.3 12.9 %collective-permute-start.2 = (bf16[2,256,256]{2,1,0:T(8,128)(2,1)S(1)}, bf16[2,256,256]{2,1,0:T(8,128)(2,1)S(1)}, u32[]{:S(2)}, u32[]{:S(2)}) collective-permute-start(bf16[2,256,256]{2,1,0:T(8,128)(2,1)S(1)} %for_across.3), channel_id=1, source_target_pairs={{0,1},{1,0},{2,3},{3,2},{4,5},{5,4},{6,7},{7,6},{8,9},{9,8},{10,11... | collective-permute-start | bytes 786440 | tf_op jit(solution)/shard_map/ppermute | solution.py:303
  61.9 10.3 %collective-permute-start.1 = (bf16[2,256,256]{2,1,0:T(8,128)(2,1)S(1)}, bf16[2,256,256]{2,1,0:T(8,128)(2,1)S(1)}, u32[]{:S(2)}, u32[]{:S(2)}) collective-permute-start(bf16[2,256,256]{2,1,0:T(8,128)(2,1)S(1)} %get-tuple-element.23.own.refs_2_.refs_6_), channel_id=1, source_target_pairs={{0,6},{1,7},{2,0},{3,1},{4,2},{5,3},{6,4},{7,5},{8,14},{9,15},{10,... | collective-permute-start | bytes 786440 | tf_op jit(solution)/shard_map/ppermute | solution.py:303
  65.6 7.2 %collective-permute-start.5 = (bf16[2,256,256]{2,1,0:T(8,128)(2,1)S(1)}, bf16[2,256,256]{2,1,0:T(8,128)(2,1)S(1)}, u32[]{:S(2)}, u32[]{:S(2)}) collective-permute-start(bf16[2,256,256]{2,1,0:T(8,128)(2,1)S(1)} %for_across.4), channel_id=1, source_target_pairs={{0,1},{1,0},{2,3},{3,2},{4,5},{5,4},{6,7},{7,6},{8,9},{9,8},{10,11... | collective-permute-start | bytes 786440 | tf_op jit(solution)/shard_map/ppermute | solution.py:303
  67.0 12.4 %collective-permute-start.13 = (bf16[2,256,256]{2,1,0:T(8,128)(2,1)S(1)}, bf16[2,256,256]{2,1,0:T(8,128)(2,1)S(1)}, u32[]{:S(2)}, u32[]{:S(2)}) collective-permute-start(bf16[2,256,256]{2,1,0:T(8,128)(2,1)S(1)} %collective-permute-done.12), channel_id=1, source_target_pairs={{0,2},{1,3},{2,4},{3,5},{4,6},{5,7},{6,0},{7,1},{8,10},{9,11},{10,... | collective-permute-start | bytes 786440 | tf_op jit(solution)/shard_map/ppermute | solution.py:303
  67.0 12.4 %collective-permute-start.14 = (bf16[2,256,256]{2,1,0:T(8,128)(2,1)S(1)}, bf16[2,256,256]{2,1,0:T(8,128)(2,1)S(1)}, u32[]{:S(2)}, u32[]{:S(2)}) collective-permute-start(bf16[2,256,256]{2,1,0:T(8,128)(2,1)S(1)} %get-tuple-element.33.refs_3_.refs_7_), channel_id=1, source_target_pairs={{0,6},{1,7},{2,0},{3,1},{4,2},{5,3},{6,4},{7,5},{8,14},{9,15},{10,... | collective-permute-start | bytes 786440 | tf_op jit(solution)/shard_map/ppermute | solution.py:303
  70.3 10.3 %collective-permute-start.11 = (bf16[2,256,256]{2,1,0:T(8,128)(2,1)S(1)}, bf16[2,256,256]{2,1,0:T(8,128)(2,1)S(1)}, u32[]{:S(2)}, u32[]{:S(2)}) collective-permute-start(bf16[2,256,256]{2,1,0:T(8,128)(2,1)S(1)} %collective-permute-done.4), channel_id=1, source_target_pairs={{0,2},{1,3},{2,4},{3,5},{4,6},{5,7},{6,0},{7,1},{8,10},{9,11},{10,... | collective-permute-start | bytes 786440 | tf_op jit(solution)/shard_map/ppermute | solution.py:303
  72.2 10.8 %collective-permute-start.9 = (bf16[2,256,256]{2,1,0:T(8,128)(2,1)S(1)}, bf16[2,256,256]{2,1,0:T(8,128)(2,1)S(1)}, u32[]{:S(2)}, u32[]{:S(2)}) collective-permute-start(bf16[2,256,256]{2,1,0:T(8,128)(2,1)S(1)} %collective-permute-done.8), channel_id=1, source_target_pairs={{0,0},{1,7},{2,2},{3,1},{4,4},{5,3},{6,6},{7,5},{8,8},{9,15},{10,1... | collective-permute-start | bytes 786440 | tf_op jit(solution)/shard_map/ppermute | solution.py:303
  72.9 13.6 %collective-permute-start.7 = (bf16[2,256,256]{2,1,0:T(8,128)(2,1)S(1)}, bf16[2,256,256]{2,1,0:T(8,128)(2,1)S(1)}, u32[]{:S(2)}, u32[]{:S(2)}) collective-permute-start(bf16[2,256,256]{2,1,0:T(8,128)(2,1)S(1)} %for_across.5), channel_id=1, source_target_pairs={{0,1},{1,0},{2,3},{3,2},{4,5},{5,4},{6,7},{7,6},{8,9},{9,8},{10,11... | collective-permute-start | bytes 786440 | tf_op jit(solution)/shard_map/ppermute | solution.py:303
  80.7 14.3 %collective-permute-start.15 = (bf16[4,256,256]{2,1,0:T(8,128)(2,1)S(1)}, bf16[4,256,256]{2,1,0:T(8,128)(2,1)S(1)}, u32[]{:S(2)}, u32[]{:S(2)}) collective-permute-start(bf16[4,256,256]{2,1,0:T(8,128)(2,1)S(1)} %pass_half.1), channel_id=1, source_target_pairs={{0,1},{1,0},{2,3},{3,2},{4,5},{5,4},{6,7},{7,6},{8,9},{9,8},{10,11... | collective-permute-start | bytes 1572872 | tf_op jit(solution)/shard_map/ppermute | solution.py:303
  81.5 10.5 %collective-permute-start.6 = (bf16[2,256,256]{2,1,0:T(8,128)(2,1)S(1)}, bf16[2,256,256]{2,1,0:T(8,128)(2,1)S(1)}, u32[]{:S(2)}, u32[]{:S(2)}) collective-permute-start(bf16[2,256,256]{2,1,0:T(8,128)(2,1)S(1)} %pass_next.2), channel_id=1, source_target_pairs={{0,6},{1,7},{2,0},{3,1},{4,2},{5,3},{6,4},{7,5},{8,14},{9,15},{10,... | collective-permute-start | bytes 786440 | tf_op jit(solution)/shard_map/ppermute | solution.py:303
  86.5 6.4 %collective-permute-start.10 = (bf16[2,256,256]{2,1,0:T(8,128)(2,1)S(1)}, bf16[2,256,256]{2,1,0:T(8,128)(2,1)S(1)}, u32[]{:S(2)}, u32[]{:S(2)}) collective-permute-start(bf16[2,256,256]{2,1,0:T(8,128)(2,1)S(1)} %pass_next.3), channel_id=1, source_target_pairs={{0,6},{1,7},{2,0},{3,1},{4,2},{5,3},{6,4},{7,5},{8,14},{9,15},{10,... | collective-permute-start | bytes 786440 | tf_op jit(solution)/shard_map/ppermute | solution.py:303
